TPU v7x, 256 devices: a whole 4x4x8 slice. The times are simulated.
256 devices in a mesh: quad: 8 (over x, z_hi), py: 8 (over y, core), pz: 4 (over z_lo).
Axes of the slice: x: 4, y: 4, z: 8 (z_hi: 2, z_lo: 4; z = z_hi * 4 + z_lo), core: 2. Of those that a mesh axis runs over, the one named last changes fastest.
Arguments:
- source_real: float32 [4, 16, 128, 512], P(None, None, 'py', 'pz'), may hold values from -6 to 6
- source_imag: float32 [4, 16, 128, 512], P(None, None, 'py', 'pz'), may hold values from -2 to 2
- potential: float32 [16, 128, 512], P(None, 'py', 'pz'), may hold values from 0 to 2
- center: float32 [1], replicated, may hold values from 4.5 to 6
- radius: float32 [1], replicated, may hold values from 1 to 2
Outputs:
- moments: float32 [4, 2, 4, 16, 128, 512], P(None, None, None, 'quad', 'py', 'pz')
All inputs are finite; a program needn't handle non-finite values.
Results may differ from a plain program's by a relative error of at most 0.0003.
Values sent between devices are 32-bit elements; how exact they have to be, the bound alone decides.
A program may use at most 128 MiB of HBM per device.

v0:
```python
import math

import jax
import jax.numpy as jnp
from jax import lax
from jax.sharding import PartitionSpec as P

QPTS = 8
MOMS = 4


stencil_weights = (-205.0 / 72.0, 8.0 / 5.0, -1.0 / 5.0, 8.0 / 315.0, -1.0 / 560.0)


def with_halo(value, sides, width):
    edges = {}
    for axis, dim in sides:
        count, length = (lax.axis_size(axis), value.shape[dim])
        up = [(i, (i + 1) % count) for i in range(count)]
        last = lax.slice_in_dim(value, length - width, length, axis=dim)
        initial = lax.slice_in_dim(value, 0, width, axis=dim)
        edges[dim] = (
            lax.ppermute(last, axis, up),
            lax.ppermute(initial, axis, [(b, a) for a, b in up]),
        )
    done = []
    for _, dim in sides:
        low, high = edges[dim]
        around = [(width, width) if d in done else (0, 0) for d in range(value.ndim)]
        value = jnp.concatenate([jnp.pad(low, around), value, jnp.pad(high, around)], axis=dim)
        done.append(dim)
    return value


def sent_to_all(value, axis):
    count = lax.axis_size(axis)
    return lax.all_to_all(
        jnp.broadcast_to(value[None], (count, *value.shape)), axis, 0, 0, tiled=True
    )


def over_copies(value, axis):
    return sent_to_all(value, axis).sum(axis=0)


def packed_total(arrays, axis):
    ends = [0]
    for a in arrays:
        ends.append(ends[-1] + a.size)
    running = over_copies(jnp.concatenate([a.ravel() for a in arrays]), axis)
    return tuple((running[b:e].reshape(a.shape) for a, b, e in zip(arrays, ends, ends[1:])))


def apply_operator(field, potential):
    padded = with_halo(field, (("py", 4), ("pz", 5)), 4)
    width_y = field.shape[4]
    width_z = field.shape[5]
    laplace = 3.0 * stencil_weights[0] * field
    for offset in range(1, 5):
        beside_all = jnp.roll(field, offset, 3) + jnp.roll(field, -offset, 3)
        beside_all = (
            beside_all + padded[:, :, :, :, 4 + offset : 4 + offset + width_y, 4 : 4 + width_z]
        )
        beside_all = (
            beside_all + padded[:, :, :, :, 4 - offset : 4 - offset + width_y, 4 : 4 + width_z]
        )
        beside_all = (
            beside_all + padded[:, :, :, :, 4 : 4 + width_y, 4 + offset : 4 + offset + width_z]
        )
        beside_all = (
            beside_all + padded[:, :, :, :, 4 : 4 + width_y, 4 - offset : 4 - offset + width_z]
        )
        laplace = laplace + stencil_weights[offset] * beside_all
    return -0.5 * laplace + potential * field


def complex_mul(left, right):
    return (left[0] * right[0] - left[1] * right[1], left[0] * right[1] + left[1] * right[0])


def complex_div(left, right):
    norm_sq = right[0] * right[0] + right[1] * right[1]
    return (
        (left[0] * right[0] + left[1] * right[1]) / norm_sq,
        (left[1] * right[0] - left[0] * right[1]) / norm_sq,
    )


def local_bilinear(left, right):
    both = complex_mul(left, right)
    return (jnp.sum(both[0], axis=(-3, -2, -1)), jnp.sum(both[1], axis=(-3, -2, -1)))


def spread(value):
    return (value[0][..., None, None, None], value[1][..., None, None, None])


def moment_terms(solution, angles, radius_value):
    orders = jnp.arange(1, MOMS + 1).astype(jnp.float32)
    phase = orders[:, None] * angles[None, :]
    weight_re = radius_value / QPTS * jnp.cos(phase)
    weight_im = radius_value / QPTS * jnp.sin(phase)
    highest = lax.Precision.HIGHEST
    real_part = jnp.einsum("kq,qsxyz->ksxyz", weight_re, solution[:, 0], precision=highest)
    real_part = real_part - jnp.einsum(
        "kq,qsxyz->ksxyz", weight_im, solution[:, 1], precision=highest
    )
    imag_part = jnp.einsum("kq,qsxyz->ksxyz", weight_re, solution[:, 1], precision=highest)
    imag_part = imag_part + jnp.einsum(
        "kq,qsxyz->ksxyz", weight_im, solution[:, 0], precision=highest
    )
    return jnp.stack([real_part, imag_part], 1)


def per_device(source_real, source_imag, potential, center, radius):
    groups = lax.axis_size("quad")
    local_count = QPTS // groups
    first_point = lax.axis_index("quad") * local_count
    indices = (first_point + jnp.arange(local_count)).astype(jnp.float32)
    angles = 2.0 * math.pi * (indices + 0.5) / QPTS
    shift_re = center[0] + radius[0] * jnp.cos(angles)
    shift_im = radius[0] * jnp.sin(angles)
    shift_pair = (shift_re[:, None], shift_im[:, None])
    shift_field = (shift_re[:, None, None, None, None], shift_im[:, None, None, None, None])
    source = (source_real, source_imag)
    applied = apply_operator(jnp.stack(source)[None], potential)[0]
    hsource = (applied[0], applied[1])
    rho_local = local_bilinear(source, source)
    curv_local = local_bilinear(source, hsource)
    totals = packed_total((rho_local[0], rho_local[1], curv_local[0], curv_local[1]), ("py", "pz"))
    rho_first = (totals[0], totals[1])
    curv_first = (totals[2], totals[3])
    scaled = complex_mul(shift_pair, rho_first)
    denom = (scaled[0] - curv_first[0], scaled[1] - curv_first[1])
    alpha_first = complex_div(rho_first, denom)
    alpha_wide = spread(alpha_first)
    first_iterate = complex_mul(alpha_wide, source)
    shifted = complex_mul(shift_field, source)
    image = (shifted[0] - hsource[0], shifted[1] - hsource[1])
    moved = complex_mul(alpha_wide, image)
    residual = (source[0] - moved[0], source[1] - moved[1])
    hres = apply_operator(jnp.stack(residual, 1), potential)
    shifted_res = complex_mul(shift_field, residual)
    image_res = (shifted_res[0] - hres[:, 0], shifted_res[1] - hres[:, 1])
    rho_part = local_bilinear(residual, residual)
    mixed_part = local_bilinear(residual, image_res)
    paired = packed_total((rho_part[0], rho_part[1], mixed_part[0], mixed_part[1]), ("py", "pz"))
    rho_next = (paired[0], paired[1])
    mixed = (paired[2], paired[3])
    beta = complex_div(rho_next, rho_first)
    carried = complex_mul(spread(beta), source)
    direction = (residual[0] + carried[0], residual[1] + carried[1])
    correction = complex_div(complex_mul(beta, rho_next), alpha_first)
    curv_next = (mixed[0] - correction[0], mixed[1] - correction[1])
    alpha_next = complex_div(rho_next, curv_next)
    step_part = complex_mul(spread(alpha_next), direction)
    solution = jnp.stack((first_iterate[0] + step_part[0], first_iterate[1] + step_part[1]), 1)
    gathered = lax.all_to_all(solution, "quad", split_axis=3, concat_axis=0, tiled=True)
    all_angles = 2.0 * math.pi * (jnp.arange(gathered.shape[0]).astype(jnp.float32) + 0.5) / QPTS
    return moment_terms(gathered, all_angles, radius[0])


def solution(mesh):
    in_specs = (P(None, None, "py", "pz"), P(None, None, "py", "pz"), P(None, "py", "pz"), P(), P())
    out_specs = P(None, None, None, "quad", "py", "pz")
    return jax.shard_map(
        per_device, mesh=mesh, in_specs=in_specs, out_specs=out_specs, check_vma=False
    )
```

profile of v0, /device:TPU:33, one launch (start us, length us, event | category | flops | bytes accessed | tf_op | source)
XLA Modules:
  0.0 176.5 jit_solution(8085165533482283820)
XLA Ops:
  0.0 1.3 pad_maximum_fusion.5
  2.5 1.9 %collective-permute-start.1 = (f32[1,2,4,16,4,128]{5,3,4,2,1,0:T(8,128)}, f32[1,2,4,16,4,128]{5,3,4,2,1,0:T(8,128)S(1)}, u32[]{:S(2)}, u32[]{:S(2)}) collective-permute-start(f32[1,2,4,16,4,128]{5,3,4,2,1,0:T(8,128)} %get-tuple-element.79), channel_id=1, source_target_pairs={{0,4},{4,8},{8,12},{12,16},{16,20},{20,24},{24,28},{28,0},{1,5},{5... | collective-permute-start | bytes 786440 | tf_op jit(solution)/shard_map/ppermute | solution.py:23
  4.7 1.6 copy.158
  6.7 1.6 copy.160
  8.3 1.3 collective-permute-start.3
  11.4 1.3 copy.156
  12.7 1.3 copy.150
  14.0 1.2 copy.151
  15.3 1.2 copy.163
  26.5 1.8 copy.222
  28.3 1.8 copy.223
  31.2 3.6 %select_maximum_fusion.3 = (f32[1,2,4,16,24,132]{5,4,3,2,1,0:T(8,128)S(1)}, f32[1,2,4,16,24,132]{5,4,3,2,1,0:T(8,128)S(1)}) fusion(f32[1,2,4,16,16,4]{5,4,3,2,1,0:T(8,128)S(1)} %copy.222, f32[1,2,4,16,4,128]{5,4,3,2,1,0:T(4,128)S(1)} %copy.157, f32[1,2,4,16,16,128]{5,4,3,2,1,0:T(8,128)} %copy.156, f32[1,2,4,16,4,128]{5,4,3,2,1,0:T(4,128)S(1)} %copy.155, ...), kind=kLoop, calls=%fused_computation.45 | loop fusion | flops 4055040 | bytes 4882432 | tf_op jit(solution)/shard_map/concatenate | solution.py:30
  34.8 4.4 %fusion.6 = (f32[1,2,4,16,16,128]{5,3,4,2,1,0:T(8,128)}, f32[1,2,4,16,16,128]{5,3,4,2,1,0:T(8,128)}, f32[1,2,4,16,16,128]{5,3,4,2,1,0:T(8,128)}, f32[1,2,4,16,16...) fusion(f32[1,2,4,16,16,128]{5,3,4,2,1,0:T(8,128)S(1)} %bitcast., ...), kind=kLoop, calls=%fused_computation.69 | loop fusion | flops 2097152 | bytes 9961472 | tf_op jit(solution)/shard_map/concatenate | solution.py:30
  39.2 10.0 %fusion.23 = f32[1,2,4,16,16,128]{5,4,3,2,1,0:T(8,128)S(1)} fusion(f32[1,2,4,16,24,132]{5,4,3,2,1,0:T(8,128)S(1)} %get-tuple-element.26, f32[1,2,4,16,24,132]{5,4,3,2,1,0:T(8,128)S(1)} %get-tuple-element.25, f32[1,2,4,15,16,128]{5,4,3,2,1,0:T(8,128)} %copy.150, f32[1,2,4,1,16,128]{5,4,3,2,1,0:T(8,128)} %bitcast.138, f32[1,2,4,1,16,128]{5,4,3,2,1,0:T(8,128)} %bitcast.137, ...), kind=kLoop, calls=%fused_computation.103 | loop fusion | flops 10747904 | bytes 27394048 | tf_op jit(solution)/shard_map/add | solution.py:74
  50.3 11.2 %all-to-all-start = ((f32[32,1,16]{2,1,0:T(1,128)}), f32[32,1,16]{2,1,0:T(1,128)S(1)}, u32[]{:S(2)}, u32[]{:S(2)}) async-start(f32[32,1,16]{2,1,0:T(1,128)} %broadcast_in_dim.7), calls=%async_computation | async-start | bytes 32768 | tf_op jit(solution)/shard_map/all_to_all | solution.py:37
  63.0 4.6 %all-to-all-done = f32[32,1,16]{2,1,0:T(1,128)S(1)} async-done(((f32[32,1,16]{2,1,0:T(1,128)}), f32[32,1,16]{2,1,0:T(1,128)S(1)}, u32[]{:S(2)}, u32[]{:S(2)}) %all-to-all-start) | async-done | bytes 2080 | tf_op jit(solution)/shard_map/all_to_all | solution.py:37
  69.6 1.3 fusion.43
  71.6 1.5 fusion.41
  73.1 1.5 fusion.39
  74.7 1.3 fusion.8
  79.3 2.8 %copy.216 = f32[1,2,4,16,16,4]{4,3,5,2,1,0:T(8,128)} copy(f32[1,2,4,16,16,4]{5,4,3,2,1,0:T(8,128)} %get-tuple-element.53) | data formatting | bytes 65536
  83.2 1.6 copy.217
  85.1 1.4 fusion.45
  87.2 3.6 %collective-permute-done.6 = f32[1,2,4,16,16,4]{4,3,5,2,1,0:T(8,128)} collective-permute-done((f32[1,2,4,16,16,4]{4,3,5,2,1,0:T(8,128)}, f32[1,2,4,16,16,4]{4,3,5,2,1,0:T(8,128)}, u32[]{:S(2)}, u32[]{:S(2)}) %collective-permute-start.6) | collective-permute-done | bytes 32800 | tf_op jit(solution)/shard_map/ppermute | solution.py:24
  90.7 1.8 copy.224
  92.5 3.9 %collective-permute-done.7 = f32[1,2,4,16,16,4]{4,3,5,2,1,0:T(8,128)} collective-permute-done((f32[1,2,4,16,16,4]{4,3,5,2,1,0:T(8,128)}, f32[1,2,4,16,16,4]{4,3,5,2,1,0:T(8,128)}, u32[]{:S(2)}, u32[]{:S(2)}) %collective-permute-start.7) | collective-permute-done | bytes 32800 | tf_op jit(solution)/shard_map/ppermute | solution.py:23
  96.4 2.7 %copy.225 = f32[1,2,4,16,16,4]{5,4,3,2,1,0:T(8,128)} copy(f32[1,2,4,16,16,4]{4,3,5,2,1,0:T(8,128)} %collective-permute-done.7) | data formatting | bytes 65536
  101.7 4.0 %select_maximum_fusion.1 = (f32[1,2,4,16,24,132]{5,4,3,2,1,0:T(8,128)}, f32[1,2,4,16,24,132]{5,4,3,2,1,0:T(8,128)}) fusion(f32[1,2,4,16,16,4]{5,4,3,2,1,0:T(8,128)S(1)} %copy.224, f32[1,2,4,16,4,128]{5,4,3,2,1,0:T(4,128)S(1)} %copy.182, f32[1,1,4,16,16,128]{5,4,3,2,1,0:T(8,128)S(1)} %bitcast.126, f32[1,1,4,16,16,128]{5,4,3,2,1,0:T(8,128)S(1)} %bitcast.113, ...), kind=kLoop, calls=%fused_computation.42 | loop fusion | flops 4866048 | bytes 4882432 | tf_op jit(solution)/shard_map/concatenate | solution.py:30
  105.7 12.7 %fusion.13 = f32[1,2,4,16,16,128]{5,4,3,2,1,0:T(8,128)S(1)} fusion(f32[1,2,4,16,24,132]{5,4,3,2,1,0:T(8,128)} %get-tuple-element.24, f32[1,2,4,16,24,132]{5,4,3,2,1,0:T(8,128)} %get-tuple-element.23, f32[1,2,4,16,20,128]{5,4,3,2,1,0:T(8,128)S(1)} %get-tuple-element.52, f32[1,2,4,16,20,128]{5,4,3,2,1,0:T(8,128)S(1)} %get-tuple-element.51, ...), kind=kLoop, calls=%fused_computation.77 | loop fusion | flops 10747904 | bytes 27394048 | tf_op jit(solution)/shard_map/add | solution.py:74
  119.0 11.9 %all_to_all.30 = f32[32,1,16]{2,1,0:T(1,128)S(1)} all-to-all(f32[32,1,16]{2,1,0:T(1,128)S(1)} %broadcast_in_dim.8), channel_id=1, replica_groups=mesh['quad'=8,'py'=8,'pz'=4] {'py','pz'}, dimensions={0} | all-to-all | bytes 4096 | tf_op jit(solution)/shard_map/all_to_all | solution.py:37
  132.9 7.9 %all-to-all-start.2 = ((f32[1,2,4,16,16,128]{5,4,2,1,0,3:T(8,128)}), f32[1,2,4,16,16,128]{5,4,2,1,0,3:T(8,128)S(1)}, u32[]{:S(2)}, u32[]{:S(2)}) async-start(f32[1,2,4,16,16,128]{5,4,2,1,0,3:T(8,128)} %copy.192), calls=%async_computation.2 | async-start | bytes 2097152 | tf_op jit(solution)/shard_map/all_to_all | solution.py:158
  140.9 31.3 %all-to-all-done.2 = f32[1,2,4,16,16,128]{5,4,2,1,0,3:T(8,128)S(1)} async-done(((f32[1,2,4,16,16,128]{5,4,2,1,0,3:T(8,128)}), f32[1,2,4,16,16,128]{5,4,2,1,0,3:T(8,128)S(1)}, u32[]{:S(2)}, u32[]{:S(2)}) %all-to-all-start.2) | async-done | bytes 1048608 | tf_op jit(solution)/shard_map/all_to_all | solution.py:158
  (79 shorter events, 33.5 us)
Async XLA Ops:
  2.5 27.6 %collective-permute-start.1 = (f32[1,2,4,16,4,128]{5,3,4,2,1,0:T(8,128)}, f32[1,2,4,16,4,128]{5,3,4,2,1,0:T(8,128)S(1)}, u32[]{:S(2)}, u32[]{:S(2)}) collective-permute-start(f32[1,2,4,16,4,128]{5,3,4,2,1,0:T(8,128)} %get-tuple-element.79), channel_id=1, source_target_pairs={{0,4},{4,8},{8,12},{12,16},{16,20},{20,24},{24,28},{28,0},{1,5},{5... | collective-permute-start | bytes 786440 | tf_op jit(solution)/shard_map/ppermute | solution.py:23
  4.3 25.8 %collective-permute-start = (f32[1,2,4,16,4,128]{5,3,4,2,1,0:T(8,128)}, f32[1,2,4,16,4,128]{5,3,4,2,1,0:T(8,128)}, u32[]{:S(2)}, u32[]{:S(2)}) collective-permute-start(f32[1,2,4,16,4,128]{5,3,4,2,1,0:T(8,128)} %get-tuple-element.80), channel_id=1, source_target_pairs={{4,0},{8,4},{12,8},{16,12},{20,16},{24,20},{28,24},{0,28},{5,1},{9... | collective-permute-start | bytes 786440 | tf_op jit(solution)/shard_map/ppermute | solution.py:24
  6.3 20.2 %collective-permute-start.2 = (f32[1,2,4,16,16,4]{4,3,5,2,1,0:T(8,128)}, f32[1,2,4,16,16,4]{4,3,5,2,1,0:T(8,128)}, u32[]{:S(2)}, u32[]{:S(2)}) collective-permute-start(f32[1,2,4,16,16,4]{4,3,5,2,1,0:T(8,128)} %copy.158), channel_id=1, source_target_pairs={{1,0},{2,1},{3,2},{0,3},{5,4},{6,5},{7,6},{4,7},{9,8},{10,9},{11,1... | collective-permute-start | bytes 98312 | tf_op jit(solution)/shard_map/ppermute | solution.py:24
  8.3 19.9 %collective-permute-start.3 = (f32[1,2,4,16,16,4]{4,3,5,2,1,0:T(8,128)}, f32[1,2,4,16,16,4]{4,3,5,2,1,0:T(8,128)}, u32[]{:S(2)}, u32[]{:S(2)}) collective-permute-start(f32[1,2,4,16,16,4]{4,3,5,2,1,0:T(8,128)} %copy.160), channel_id=1, source_target_pairs={{0,1},{1,2},{2,3},{3,0},{4,5},{5,6},{6,7},{7,4},{8,9},{9,10},{10,1... | collective-permute-start | bytes 98312 | tf_op jit(solution)/shard_map/ppermute | solution.py:23
  34.8 4.4 %copy-start = (f32[4,16,16,128]{3,2,1,0:T(8,128)S(1)}, f32[4,16,16,128]{3,2,1,0:T(8,128)}, u32[]{:S(2)}) copy-start(f32[4,16,16,128]{3,2,1,0:T(8,128)} %param.5) | copy-start | bytes 1572868
  34.8 4.4 %copy-start.1 = (f32[4,16,16,128]{3,2,1,0:T(8,128)S(1)}, f32[4,16,16,128]{3,2,1,0:T(8,128)}, u32[]{:S(2)}) copy-start(f32[4,16,16,128]{3,2,1,0:T(8,128)} %param.6) | copy-start | bytes 1572868
  34.8 4.4 %copy-start.3 = (f32[16,16,128]{2,1,0:T(8,128)S(1)}, f32[16,16,128]{2,1,0:T(8,128)}, u32[]{:S(2)}) copy-start(f32[16,16,128]{2,1,0:T(8,128)} %param.7) | copy-start | bytes 393220
  50.3 17.3 %all-to-all-start = ((f32[32,1,16]{2,1,0:T(1,128)}), f32[32,1,16]{2,1,0:T(1,128)S(1)}, u32[]{:S(2)}, u32[]{:S(2)}) async-start(f32[32,1,16]{2,1,0:T(1,128)} %broadcast_in_dim.7), calls=%async_computation | async-start | bytes 32768 | tf_op jit(solution)/shard_map/all_to_all | solution.py:37
  76.8 22.3 %collective-permute-start.4 = (f32[1,2,4,16,4,128]{5,3,4,2,1,0:T(8,128)}, f32[1,2,4,16,4,128]{5,3,4,2,1,0:T(8,128)}, u32[]{:S(2)}, u32[]{:S(2)}) collective-permute-start(f32[1,2,4,16,4,128]{5,3,4,2,1,0:T(8,128)} %copy.214), channel_id=1, source_target_pairs={{4,0},{8,4},{12,8},{16,12},{20,16},{24,20},{28,24},{0,28},{5,1},{9... | collective-permute-start | bytes 786440 | tf_op jit(solution)/shard_map/ppermute | solution.py:24
  78.1 22.1 %collective-permute-start.5 = (f32[1,2,4,16,4,128]{5,3,4,2,1,0:T(8,128)}, f32[1,2,4,16,4,128]{5,3,4,2,1,0:T(8,128)}, u32[]{:S(2)}, u32[]{:S(2)}) collective-permute-start(f32[1,2,4,16,4,128]{5,3,4,2,1,0:T(8,128)} %copy.215), channel_id=1, source_target_pairs={{0,4},{4,8},{8,12},{12,16},{16,20},{20,24},{24,28},{28,0},{1,5},{5... | collective-permute-start | bytes 786440 | tf_op jit(solution)/shard_map/ppermute | solution.py:23
  82.1 8.6 %collective-permute-start.6 = (f32[1,2,4,16,16,4]{4,3,5,2,1,0:T(8,128)}, f32[1,2,4,16,16,4]{4,3,5,2,1,0:T(8,128)}, u32[]{:S(2)}, u32[]{:S(2)}) collective-permute-start(f32[1,2,4,16,16,4]{4,3,5,2,1,0:T(8,128)} %copy.216), channel_id=1, source_target_pairs={{1,0},{2,1},{3,2},{0,3},{5,4},{6,5},{7,6},{4,7},{9,8},{10,9},{11,1... | collective-permute-start | bytes 98312 | tf_op jit(solution)/shard_map/ppermute | solution.py:24
  84.8 11.6 %collective-permute-start.7 = (f32[1,2,4,16,16,4]{4,3,5,2,1,0:T(8,128)}, f32[1,2,4,16,16,4]{4,3,5,2,1,0:T(8,128)}, u32[]{:S(2)}, u32[]{:S(2)}) collective-permute-start(f32[1,2,4,16,16,4]{4,3,5,2,1,0:T(8,128)} %copy.217), channel_id=1, source_target_pairs={{0,1},{1,2},{2,3},{3,0},{4,5},{5,6},{6,7},{7,4},{8,9},{9,10},{10,1... | collective-permute-start | bytes 98312 | tf_op jit(solution)/shard_map/ppermute | solution.py:23
  99.1 2.6 %copy-start.2 = (f32[1,2,4,16,16,4]{5,4,3,2,1,0:T(8,128)S(1)}, f32[1,2,4,16,16,4]{5,4,3,2,1,0:T(8,128)}, u32[]{:S(2)}) copy-start(f32[1,2,4,16,16,4]{5,4,3,2,1,0:T(8,128)} %copy.225) | copy-start | bytes 98308
  132.9 39.3 %all-to-all-start.2 = ((f32[1,2,4,16,16,128]{5,4,2,1,0,3:T(8,128)}), f32[1,2,4,16,16,128]{5,4,2,1,0,3:T(8,128)S(1)}, u32[]{:S(2)}, u32[]{:S(2)}) async-start(f32[1,2,4,16,16,128]{5,4,2,1,0,3:T(8,128)} %copy.192), calls=%async_computation.2 | async-start | bytes 2097152 | tf_op jit(solution)/shard_map/all_to_all | solution.py:158
where the time goes:
time: 177 us
  other arithmetic  48.8 us (28%)
  waiting for transfers between devices  43.3 us (24%)
  local copies, waits for them, and re-layouts  42.1 us (24%)
  starting transfers between devices  25.8 us (15%)
  blocking collectives  11.9 us (7%)
  matrix products  2.71 us (2%)
    all_to_all x1, waiting for transfers between devices, per_device(): lax.all_to_all(solution, 'quad', split_axis=3, concat_axis=0, tiled=True)  31.3 us
    add x2, other arithmetic, apply_operator(): return -0.5 * laplace + potential * field  22.7 us
    slice x22, local copies, waits for them, and re-layouts, apply_operator(): beside_all = jnp.roll(field, offset, 3) + jnp.roll(field, -offset, 3)  15.5 us
    unnamed x16, local copies, waits for them, and re-layouts  13.9 us
    concatenate x4, other arithmetic, with_halo(): jnp.concatenate([jnp.pad(low, around), value, jnp.pad(high, around)], axi...  12.3 us
    all_to_all x1, blocking collectives, sent_to_all(): lax.all_to_all(jnp.broadcast_to(value[None], (count, *value.shape)), axis...  11.9 us
    all_to_all x1, starting transfers between devices, sent_to_all(): lax.all_to_all(jnp.broadcast_to(value[None], (count, *value.shape)), axis...  11.2 us
    another operation x10, other arithmetic, per_device(): hres = apply_operator(jnp.stack(residual, 1), potential)  10.1 us
  transfers between devices with their start and end apart: 10, of which 4 were waited for; matrix products, arithmetic and copies ran while one was open for 21% of the time, Pallas kernels for 0%

commit v1 on v0

v1 whole, which is shorter than its diff:
```python
import math

import jax
import jax.numpy as jnp
from jax import lax
from jax.sharding import PartitionSpec as P

QPTS = 8
MOMS = 4


stencil_weights = (-205.0 / 72.0, 8.0 / 5.0, -1.0 / 5.0, 8.0 / 315.0, -1.0 / 560.0)


def with_halo(value, sides, width):
    edges = {}
    for axis, dim in sides:
        count, length = (lax.axis_size(axis), value.shape[dim])
        up = [(i, (i + 1) % count) for i in range(count)]
        last = lax.slice_in_dim(value, length - width, length, axis=dim)
        initial = lax.slice_in_dim(value, 0, width, axis=dim)
        edges[dim] = (
            lax.ppermute(last, axis, up),
            lax.ppermute(initial, axis, [(b, a) for a, b in up]),
        )
    done = []
    for _, dim in sides:
        low, high = edges[dim]
        around = [(width, width) if d in done else (0, 0) for d in range(value.ndim)]
        value = jnp.concatenate([jnp.pad(low, around), value, jnp.pad(high, around)], axis=dim)
        done.append(dim)
    return value


def sent_to_all(value, axis):
    count = lax.axis_size(axis)
    return lax.all_to_all(
        jnp.broadcast_to(value[None], (count, *value.shape)), axis, 0, 0, tiled=True
    )


def over_copies(value, axis):
    return sent_to_all(value, axis).sum(axis=0)


def packed_total(arrays, axis):
    ends = [0]
    for a in arrays:
        ends.append(ends[-1] + a.size)
    running = over_copies(jnp.concatenate([a.ravel() for a in arrays]), axis)
    return tuple((running[b:e].reshape(a.shape) for a, b, e in zip(arrays, ends, ends[1:])))


def apply_operator(field, potential):
    padded = with_halo(field, (("py", 4), ("pz", 5)), 4)
    width_y = field.shape[4]
    width_z = field.shape[5]
    laplace = 3.0 * stencil_weights[0] * field
    for offset in range(1, 5):
        beside_all = jnp.roll(field, offset, 3) + jnp.roll(field, -offset, 3)
        beside_all = (
            beside_all + padded[:, :, :, :, 4 + offset : 4 + offset + width_y, 4 : 4 + width_z]
        )
        beside_all = (
            beside_all + padded[:, :, :, :, 4 - offset : 4 - offset + width_y, 4 : 4 + width_z]
        )
        beside_all = (
            beside_all + padded[:, :, :, :, 4 : 4 + width_y, 4 + offset : 4 + offset + width_z]
        )
        beside_all = (
            beside_all + padded[:, :, :, :, 4 : 4 + width_y, 4 - offset : 4 - offset + width_z]
        )
        laplace = laplace + stencil_weights[offset] * beside_all
    return -0.5 * laplace + potential * field


def complex_mul(left, right):
    return (left[0] * right[0] - left[1] * right[1], left[0] * right[1] + left[1] * right[0])


def complex_div(left, right):
    norm_sq = right[0] * right[0] + right[1] * right[1]
    return (
        (left[0] * right[0] + left[1] * right[1]) / norm_sq,
        (left[1] * right[0] - left[0] * right[1]) / norm_sq,
    )


def local_bilinear(left, right):
    both = complex_mul(left, right)
    return (jnp.sum(both[0], axis=(-3, -2, -1)), jnp.sum(both[1], axis=(-3, -2, -1)))


def spread(value):
    return (value[0][..., None, None, None], value[1][..., None, None, None])


def recip(value):
    return complex_div((jnp.ones_like(value[0]), jnp.zeros_like(value[0])), value)


def coefficients(totals, radius_value):
    mu0, mu1, mu2, mu3 = totals
    tau = complex_div(mu1, mu0)
    tau_mu1 = complex_mul(tau, mu1)
    nu2 = (mu2[0] - tau_mu1[0], mu2[1] - tau_mu1[1])
    tau_mu2 = complex_mul(tau, mu2)
    tau2_mu1 = complex_mul(tau, tau_mu1)
    nu3 = (mu3[0] - 2.0 * tau_mu2[0] + tau2_mu1[0], mu3[1] - 2.0 * tau_mu2[1] + tau2_mu1[1])
    ratio = complex_div(nu3, nu2)
    slope = complex_div(nu2, mu0)
    angles = 2.0 * math.pi * (jnp.arange(QPTS).astype(jnp.float32)[:, None] + 0.5) / QPTS
    shift = (radius_value * jnp.cos(angles), radius_value * jnp.sin(angles))
    alpha_first = recip((shift[0] - tau[0], shift[1] - tau[1]))
    gamma = complex_mul(alpha_first, slope)
    alpha_next = recip((shift[0] - ratio[0] - gamma[0], shift[1] - ratio[1] - gamma[1]))
    image_part = complex_mul(alpha_first, alpha_next)
    back = complex_mul(image_part, (gamma[0] - tau[0], gamma[1] - tau[1]))
    source_part = (alpha_first[0] + back[0], alpha_first[1] + back[1])
    orders = jnp.arange(1, MOMS + 1).astype(jnp.float32)
    phase = orders[:, None, None] * angles[None]
    weight = (radius_value / QPTS * jnp.cos(phase), radius_value / QPTS * jnp.sin(phase))
    out = []
    for part in (source_part, image_part):
        both = complex_mul(weight, (part[0][None], part[1][None]))
        out.append((jnp.sum(both[0], 1), jnp.sum(both[1], 1)))
    return out


def per_device(source_real, source_imag, potential, center, radius):
    source = jnp.stack((source_real, source_imag))
    shifted = potential - center[0]
    image = apply_operator(source[None], shifted)[0]
    image_two = apply_operator(image[None], shifted)[0]
    pairs = ((source, source), (source, image), (image, image), (image, image_two))
    parts = [local_bilinear((u[0], u[1]), (v[0], v[1])) for u, v in pairs]
    totals = packed_total([p for pair in parts for p in pair], ("py", "pz"))
    totals = [(totals[2 * i], totals[2 * i + 1]) for i in range(4)]
    source_weight, image_weight = coefficients(totals, radius[0])
    count = source_real.shape[1] // lax.axis_size("quad")
    first = lax.axis_index("quad") * count
    own = lax.dynamic_slice_in_dim(source, first, count, 2)
    own_image = lax.dynamic_slice_in_dim(image, first, count, 2)
    a = complex_mul(spread(source_weight), (own[0], own[1]))
    b = complex_mul(spread(image_weight), (own_image[0], own_image[1]))
    return jnp.stack([a[0] + b[0], a[1] + b[1]], 1)


def solution(mesh):
    in_specs = (P(None, None, "py", "pz"), P(None, None, "py", "pz"), P(None, "py", "pz"), P(), P())
    out_specs = P(None, None, None, "quad", "py", "pz")
    return jax.shard_map(
        per_device, mesh=mesh, in_specs=in_specs, out_specs=out_specs, check_vma=False
    )
```

time: 177 us -> 100 us (0.56)
  the two profiles are of different devices: /device:TPU:33 before, /device:TPU:1 now
where the time goes in v1:
time: 100 us; the launch traced here: 99.7 us
  local copies, waits for them, and re-layouts  41.2 us (41%)
  starting transfers between devices  22.2 us (22%)
  other arithmetic  21.4 us (21%)
  waiting for transfers between devices  13.2 us (13%)
  between operations  1.71 us (2%)
    slice x16, local copies, waits for them, and re-layouts, apply_operator(): beside_all = jnp.roll(field, offset, 3) + jnp.roll(field, -offset, 3)  19 us
    ppermute x4, starting transfers between devices, with_halo(): lax.ppermute(initial, axis, [(b, a) for a, b in up])  11.9 us
    all_to_all x1, starting transfers between devices, sent_to_all(): lax.all_to_all(jnp.broadcast_to(value[None], (count, *value.shape)), axis...  10 us
    add x2, other arithmetic, apply_operator(): return -0.5 * laplace + potential * field  9.9 us
    slice x6, local copies, waits for them, and re-layouts, with_halo(): initial = lax.slice_in_dim(value, 0, width, axis=dim)  7.88 us
    all_to_all x1, waiting for transfers between devices, sent_to_all(): lax.all_to_all(jnp.broadcast_to(value[None], (count, *value.shape)), axis...  7.04 us
    concatenate x2, other arithmetic, with_halo(): jnp.concatenate([jnp.pad(low, around), value, jnp.pad(high, around)], axi...  5.73 us
    ppermute x2, local copies, waits for them, and re-layouts, with_halo(): lax.ppermute(last, axis, up)  5.59 us
  transfers between devices with their start and end apart: 9, of which 3 were waited for; matrix products, arithmetic and copies ran while one was open for 31% of the time, Pallas kernels for 0%

profile of v1, /device:TPU:1, one launch (start us, length us, event | category | flops | bytes accessed | tf_op | source)
XLA Modules:
  0.0 99.7 jit_solution(3787867296911892707)
XLA Ops:
  0.0 1.3 %pad_maximum_fusion = f32[2,4,16,16,128]{4,3,2,1,0:T(8,128)S(1)} fusion(f32[1,4,16,16,128]{4,3,2,1,0:T(8,128)} %bitcast.73, f32[1,4,16,16,128]{4,3,2,1,0:T(8,128)} %bitcast.76), kind=kLoop, calls=%fused_computation.31 | loop fusion | flops 262144 | bytes 2097152 | tf_op jit(solution)/shard_map/stack | solution.py:131
  2.4 3.2 %collective-permute-start = (f32[1,2,4,16,4,128]{5,3,4,2,1,0:T(8,128)}, f32[1,2,4,16,4,128]{5,3,4,2,1,0:T(8,128)S(1)}, u32[]{:S(2)}, u32[]{:S(2)}) collective-permute-start(f32[1,2,4,16,4,128]{5,3,4,2,1,0:T(8,128)} %get-tuple-element.73), channel_id=1, source_target_pairs={{4,0},{8,4},{12,8},{16,12},{20,16},{24,20},{28,24},{0,28},{5,1},{9... | collective-permute-start | bytes 786440 | tf_op jit(solution)/shard_map/ppermute | solution.py:24
  6.0 1.6 %copy.166 = f32[1,2,4,16,16,4]{4,3,5,2,1,0:T(8,128)} copy(f32[1,2,4,16,16,4]{5,3,4,2,1,0:T(8,128)S(1)} %get-tuple-element.71) | data formatting | bytes 65536 | tf_op jit(solution)/shard_map/slice | solution.py:21
  7.7 3.8 %collective-permute-start.2 = (f32[1,2,4,16,16,4]{4,3,5,2,1,0:T(8,128)}, f32[1,2,4,16,16,4]{4,3,5,2,1,0:T(8,128)}, u32[]{:S(2)}, u32[]{:S(2)}) collective-permute-start(f32[1,2,4,16,16,4]{4,3,5,2,1,0:T(8,128)} %copy.166), channel_id=1, source_target_pairs={{1,0},{2,1},{3,2},{0,3},{5,4},{6,5},{7,6},{4,7},{9,8},{10,9},{11,1... | collective-permute-start | bytes 98312 | tf_op jit(solution)/shard_map/ppermute | solution.py:24
  11.4 1.6 %copy.168 = f32[1,2,4,16,16,4]{4,3,5,2,1,0:T(8,128)} copy(f32[1,2,4,16,16,4]{5,3,4,2,1,0:T(8,128)S(1)} %get-tuple-element.72) | data formatting | bytes 65536 | tf_op jit(solution)/shard_map/slice | solution.py:20
  13.1 1.5 %fusion.77 = (f32[1,2,4,12,16,128]{5,3,4,2,1,0:T(8,128)}, f32[1,2,4,12,16,128]{5,3,4,2,1,0:T(8,128)}) fusion(f32[1,2,4,16,16,128]{5,3,4,2,1,0:T(8,128)S(1)} %bitcast.63), kind=kLoop, calls=%fused_computation.188 | loop fusion | bytes 3145728 | tf_op jit(solution)/shard_map/jit(_roll_static)/slice | solution.py:60
  14.6 1.6 %fusion.79 = (f32[1,2,4,13,16,128]{5,3,4,2,1,0:T(8,128)}, f32[1,2,4,13,16,128]{5,3,4,2,1,0:T(8,128)}) fusion(f32[1,2,4,16,16,128]{5,3,4,2,1,0:T(8,128)S(1)} %bitcast.64), kind=kLoop, calls=%fused_computation.190 | loop fusion | bytes 3407872 | tf_op jit(solution)/shard_map/jit(_roll_static)/slice | solution.py:60
  16.2 1.5 %fusion.81 = (f32[1,2,4,14,16,128]{5,3,4,2,1,0:T(8,128)}, f32[1,2,4,14,16,128]{5,3,4,2,1,0:T(8,128)}) fusion(f32[1,2,4,16,16,128]{5,3,4,2,1,0:T(8,128)S(1)} %bitcast.65), kind=kLoop, calls=%fused_computation.192 | loop fusion | bytes 3670016 | tf_op jit(solution)/shard_map/jit(_roll_static)/slice | solution.py:60
  17.7 1.5 %fusion.83 = (f32[1,2,4,15,16,128]{5,3,4,2,1,0:T(8,128)}, f32[1,2,4,15,16,128]{5,3,4,2,1,0:T(8,128)}) fusion(f32[1,2,4,16,16,128]{5,3,4,2,1,0:T(8,128)S(1)} %bitcast.66), kind=kLoop, calls=%fused_computation.194 | loop fusion | bytes 3932160 | tf_op jit(solution)/shard_map/jit(_roll_static)/slice | solution.py:60
  24.6 1.1 %pad_maximum_fusion.5 = f32[1,2,4,16,16,128]{5,4,3,2,1,0:T(8,128)} fusion(f32[1,1,4,16,16,128]{5,4,3,2,1,0:T(8,128)S(1)} %bitcast.75, f32[1,1,4,16,16,128]{5,4,3,2,1,0:T(8,128)S(1)} %bitcast.78), kind=kLoop, calls=%fused_computation.101 | loop fusion | flops 262144 | bytes 2097152 | tf_op jit(solution)/shard_map/stack | solution.py:131
  26.8 1.8 %copy.167 = f32[1,2,4,16,16,4]{5,3,4,2,1,0:T(8,128)S(1)} copy(f32[1,2,4,16,16,4]{4,3,5,2,1,0:T(8,128)} %collective-permute-done.2) | data formatting | bytes 65536 | tf_op jit(solution)/shard_map/ppermute | solution.py:24
  28.6 2.8 %copy.169 = f32[1,2,4,16,16,4]{5,3,4,2,1,0:T(8,128)} copy(f32[1,2,4,16,16,4]{4,3,5,2,1,0:T(8,128)} %collective-permute-done.3) | data formatting | bytes 65536 | tf_op jit(solution)/shard_map/ppermute | solution.py:23
  31.4 2.9 %select_maximum_fusion.3 = (f32[1,2,4,16,24,132]{5,3,4,2,1,0:T(8,128)S(1)}, f32[1,2,4,16,24,132]{5,3,4,2,1,0:T(8,128)S(1)}) fusion(f32[1,2,4,16,16,4]{5,3,4,2,1,0:T(8,128)S(1)} %copy.167, f32[1,2,4,16,4,128]{5,3,4,2,1,0:T(8,128)S(1)} %collective-permute-done, f32[1,2,4,16,16,128]{5,3,4,2,1,0:T(8,128)S(1)} %bitcast.71, ...), kind=kLoop, calls=%fused_computation.4 | loop fusion | flops 4055040 | bytes 4882432 | tf_op jit(solution)/shard_map/concatenate | solution.py:30
  34.3 5.0 %fusion.35 = f32[1,2,4,16,16,128]{5,3,4,2,1,0:T(8,128)S(1)} fusion(f32[1,2,4,16,16,128]{5,3,4,2,1,0:T(8,128)S(1)} %bitcast.72, f32[1,2,4,16,4,128]{5,3,4,2,1,0:T(8,128)} %collective-permute-done.1, f32[1,2,4,16,4,128]{5,3,4,2,1,0:T(8,128)S(1)} %collective-permute-done, f32[1,2,4,16,24,132]{5,3,4,2,1,0:T(8,128)S(1)} %get-tuple-element.32, ...), kind=kLoop, calls=%fused_computation.68 | loop fusion | flops 12582912 | bytes 20578304 | tf_op jit(solution)/shard_map/add | solution.py:74
  39.4 1.4 %fusion.75 = (f32[1,2,4,16,16,4]{5,3,4,2,1,0:T(8,128)}, f32[1,2,4,16,16,4]{5,3,4,2,1,0:T(8,128)S(1)}) fusion(f32[1,2,4,16,16,128]{5,3,4,2,1,0:T(8,128)S(1)} %fusion.35), kind=kLoop, calls=%fused_computation.186 | loop fusion | bytes 131072 | tf_op jit(solution)/shard_map/slice | solution.py:21
  41.6 1.5 %fusion.67 = (f32[1,2,4,12,16,128]{5,3,4,2,1,0:T(8,128)}, f32[1,2,4,12,16,128]{5,3,4,2,1,0:T(8,128)}) fusion(f32[1,2,4,16,16,128]{5,3,4,2,1,0:T(8,128)S(1)} %fusion.35), kind=kLoop, calls=%fused_computation.178 | loop fusion | bytes 3145728 | tf_op jit(solution)/shard_map/jit(_roll_static)/slice | solution.py:60
  43.2 1.6 %fusion.69 = (f32[1,2,4,13,16,128]{5,3,4,2,1,0:T(8,128)}, f32[1,2,4,13,16,128]{5,3,4,2,1,0:T(8,128)}) fusion(f32[1,2,4,16,16,128]{5,3,4,2,1,0:T(8,128)S(1)} %fusion.35), kind=kLoop, calls=%fused_computation.180 | loop fusion | bytes 3407872 | tf_op jit(solution)/shard_map/jit(_roll_static)/slice | solution.py:60
  44.7 1.5 %fusion.71 = (f32[1,2,4,14,16,128]{5,3,4,2,1,0:T(8,128)}, f32[1,2,4,14,16,128]{5,3,4,2,1,0:T(8,128)}) fusion(f32[1,2,4,16,16,128]{5,3,4,2,1,0:T(8,128)S(1)} %fusion.35), kind=kLoop, calls=%fused_computation.182 | loop fusion | bytes 3670016 | tf_op jit(solution)/shard_map/jit(_roll_static)/slice | solution.py:60
  46.2 1.5 %fusion.73 = (f32[1,2,4,15,16,128]{5,3,4,2,1,0:T(8,128)}, f32[1,2,4,15,16,128]{5,3,4,2,1,0:T(8,128)}) fusion(f32[1,2,4,16,16,128]{5,3,4,2,1,0:T(8,128)S(1)} %fusion.35), kind=kLoop, calls=%fused_computation.184 | loop fusion | bytes 3932160 | tf_op jit(solution)/shard_map/jit(_roll_static)/slice | solution.py:60
  47.8 0.9 fusion.68
  49.6 1.6 %collective-permute-start.4 = (f32[1,2,4,16,4,128]{5,3,4,2,1,0:T(8,128)}, f32[1,2,4,16,4,128]{5,3,4,2,1,0:T(8,128)S(1)}, u32[]{:S(2)}, u32[]{:S(2)}) collective-permute-start(f32[1,2,4,16,4,128]{5,3,4,2,1,0:T(8,128)} %get-tuple-element.53), channel_id=1, source_target_pairs={{4,0},{8,4},{12,8},{16,12},{20,16},{24,20},{28,24},{0,28},{5,1},{9... | collective-permute-start | bytes 786440 | tf_op jit(solution)/shard_map/ppermute | solution.py:24
  52.2 2.8 %copy.176 = f32[1,2,4,16,16,4]{4,3,5,2,1,0:T(8,128)} copy(f32[1,2,4,16,16,4]{5,3,4,2,1,0:T(8,128)} %get-tuple-element.51) | data formatting | bytes 65536 | tf_op jit(solution)/shard_map/slice | solution.py:21
  55.0 3.4 %collective-permute-start.6 = (f32[1,2,4,16,16,4]{4,3,5,2,1,0:T(8,128)}, f32[1,2,4,16,16,4]{4,3,5,2,1,0:T(8,128)}, u32[]{:S(2)}, u32[]{:S(2)}) collective-permute-start(f32[1,2,4,16,16,4]{4,3,5,2,1,0:T(8,128)} %copy.176), channel_id=1, source_target_pairs={{1,0},{2,1},{3,2},{0,3},{5,4},{6,5},{7,6},{4,7},{9,8},{10,9},{11,1... | collective-permute-start | bytes 98312 | tf_op jit(solution)/shard_map/ppermute | solution.py:24
  58.3 1.6 %copy.178 = f32[1,2,4,16,16,4]{4,3,5,2,1,0:T(8,128)} copy(f32[1,2,4,16,16,4]{5,3,4,2,1,0:T(8,128)S(1)} %get-tuple-element.52) | data formatting | bytes 65536 | tf_op jit(solution)/shard_map/slice | solution.py:20
  60.7 1.3 %collective-permute-done.6 = f32[1,2,4,16,16,4]{4,3,5,2,1,0:T(8,128)} collective-permute-done((f32[1,2,4,16,16,4]{4,3,5,2,1,0:T(8,128)}, f32[1,2,4,16,16,4]{4,3,5,2,1,0:T(8,128)}, u32[]{:S(2)}, u32[]{:S(2)}) %collective-permute-start.6) | collective-permute-done | bytes 32800 | tf_op jit(solution)/shard_map/ppermute | solution.py:24
  62.0 1.8 %copy.177 = f32[1,2,4,16,16,4]{5,3,4,2,1,0:T(8,128)S(1)} copy(f32[1,2,4,16,16,4]{4,3,5,2,1,0:T(8,128)} %collective-permute-done.6) | data formatting | bytes 65536 | tf_op jit(solution)/shard_map/ppermute | solution.py:24
  63.8 4.9 %collective-permute-done.7 = f32[1,2,4,16,16,4]{4,3,5,2,1,0:T(8,128)} collective-permute-done((f32[1,2,4,16,16,4]{4,3,5,2,1,0:T(8,128)}, f32[1,2,4,16,16,4]{4,3,5,2,1,0:T(8,128)}, u32[]{:S(2)}, u32[]{:S(2)}) %collective-permute-start.7) | collective-permute-done | bytes 32800 | tf_op jit(solution)/shard_map/ppermute | solution.py:23
  68.6 2.8 %copy.179 = f32[1,2,4,16,16,4]{5,3,4,2,1,0:T(8,128)} copy(f32[1,2,4,16,16,4]{4,3,5,2,1,0:T(8,128)} %collective-permute-done.7) | data formatting | bytes 65536 | tf_op jit(solution)/shard_map/ppermute | solution.py:23
  71.5 2.9 %select_maximum_fusion.1 = (f32[1,2,4,16,24,132]{5,3,4,2,1,0:T(8,128)S(1)}, f32[1,2,4,16,24,132]{5,3,4,2,1,0:T(8,128)S(1)}) fusion(f32[1,2,4,16,16,4]{5,3,4,2,1,0:T(8,128)S(1)} %copy.177, f32[1,2,4,16,4,128]{5,3,4,2,1,0:T(8,128)S(1)} %collective-permute-done.4, f32[1,2,4,16,16,128]{5,3,4,2,1,0:T(8,128)S(1)} %fusion.35, ...), kind=kLoop, calls=%fused_computation.1 | loop fusion | flops 4055040 | bytes 4882432 | tf_op jit(solution)/shard_map/concatenate | solution.py:30
  74.5 4.9 %fusion.8 = f32[1,2,4,16,16,128]{5,3,4,2,1,0:T(8,128)S(1)} fusion(f32[1,2,4,16,16,128]{5,3,4,2,1,0:T(8,128)S(1)} %fusion.35, f32[1,2,4,16,4,128]{5,3,4,2,1,0:T(8,128)} %collective-permute-done.5, f32[1,2,4,16,4,128]{5,3,4,2,1,0:T(8,128)S(1)} %collective-permute-done.4, f32[1,2,4,16,24,132]{5,3,4,2,1,0:T(8,128)S(1)} %get-tuple-element.30, ...), kind=kLoop, calls=%fused_computation.41 | loop fusion | flops 12582912 | bytes 19529728 | tf_op jit(solution)/shard_map/add | solution.py:74
  81.0 10.0 %all-to-all-start = ((f32[32,1,32]{2,1,0:T(1,128)}), f32[32,1,32]{2,1,0:T(1,128)S(1)}, u32[]{:S(2)}, u32[]{:S(2)}) async-start(f32[32,1,32]{2,1,0:T(1,128)} %broadcast_in_dim.5), calls=%async_computation | async-start | bytes 32768 | tf_op jit(solution)/shard_map/all_to_all | solution.py:37
  91.1 7.0 %all-to-all-done = f32[32,1,32]{2,1,0:T(1,128)S(1)} async-done(((f32[32,1,32]{2,1,0:T(1,128)}), f32[32,1,32]{2,1,0:T(1,128)S(1)}, u32[]{:S(2)}, u32[]{:S(2)}) %all-to-all-start) | async-done | bytes 4128 | tf_op jit(solution)/shard_map/all_to_all | solution.py:37
  (84 shorter events, 13.3 us)
Async XLA Ops:
  2.4 28.9 %collective-permute-start = (f32[1,2,4,16,4,128]{5,3,4,2,1,0:T(8,128)}, f32[1,2,4,16,4,128]{5,3,4,2,1,0:T(8,128)S(1)}, u32[]{:S(2)}, u32[]{:S(2)}) collective-permute-start(f32[1,2,4,16,4,128]{5,3,4,2,1,0:T(8,128)} %get-tuple-element.73), channel_id=1, source_target_pairs={{4,0},{8,4},{12,8},{16,12},{20,16},{24,20},{28,24},{0,28},{5,1},{9... | collective-permute-start | bytes 786440 | tf_op jit(solution)/shard_map/ppermute | solution.py:24
  5.7 25.7 %collective-permute-start.1 = (f32[1,2,4,16,4,128]{5,3,4,2,1,0:T(8,128)}, f32[1,2,4,16,4,128]{5,3,4,2,1,0:T(8,128)}, u32[]{:S(2)}, u32[]{:S(2)}) collective-permute-start(f32[1,2,4,16,4,128]{5,3,4,2,1,0:T(8,128)} %get-tuple-element.74), channel_id=1, source_target_pairs={{0,4},{4,8},{8,12},{12,16},{16,20},{20,24},{24,28},{28,0},{1,5},{5... | collective-permute-start | bytes 786440 | tf_op jit(solution)/shard_map/ppermute | solution.py:23
  7.7 19.1 %collective-permute-start.2 = (f32[1,2,4,16,16,4]{4,3,5,2,1,0:T(8,128)}, f32[1,2,4,16,16,4]{4,3,5,2,1,0:T(8,128)}, u32[]{:S(2)}, u32[]{:S(2)}) collective-permute-start(f32[1,2,4,16,16,4]{4,3,5,2,1,0:T(8,128)} %copy.166), channel_id=1, source_target_pairs={{1,0},{2,1},{3,2},{0,3},{5,4},{6,5},{7,6},{4,7},{9,8},{10,9},{11,1... | collective-permute-start | bytes 98312 | tf_op jit(solution)/shard_map/ppermute | solution.py:24
  13.1 15.5 %collective-permute-start.3 = (f32[1,2,4,16,16,4]{4,3,5,2,1,0:T(8,128)}, f32[1,2,4,16,16,4]{4,3,5,2,1,0:T(8,128)}, u32[]{:S(2)}, u32[]{:S(2)}) collective-permute-start(f32[1,2,4,16,16,4]{4,3,5,2,1,0:T(8,128)} %copy.168), channel_id=1, source_target_pairs={{0,1},{1,2},{2,3},{3,0},{4,5},{5,6},{6,7},{7,4},{8,9},{9,10},{10,1... | collective-permute-start | bytes 98312 | tf_op jit(solution)/shard_map/ppermute | solution.py:23
  17.7 6.2 %copy-start = (f32[4,16,16,128]{3,2,1,0:T(8,128)S(1)}, f32[4,16,16,128]{3,2,1,0:T(8,128)}, u32[]{:S(2)}) copy-start(f32[4,16,16,128]{3,2,1,0:T(8,128)} %param.6) | copy-start | bytes 1572868
  17.7 6.2 %copy-start.1 = (f32[4,16,16,128]{3,2,1,0:T(8,128)S(1)}, f32[4,16,16,128]{3,2,1,0:T(8,128)}, u32[]{:S(2)}) copy-start(f32[4,16,16,128]{3,2,1,0:T(8,128)} %param.5) | copy-start | bytes 1572868
  19.2 5.4 %copy-start.17 = (f32[16,16,128]{2,1,0:T(8,128)S(1)}, f32[16,16,128]{2,1,0:T(8,128)}, u32[]{:S(2)}) copy-start(f32[16,16,128]{2,1,0:T(8,128)} %param.7) | copy-start | bytes 393220
  31.3 2.9 %copy-start.5 = (f32[1,2,4,16,16,128]{5,4,3,2,1,0:T(8,128)S(1)}, f32[1,2,4,16,16,128]{5,4,3,2,1,0:T(8,128)}, u32[]{:S(2)}) copy-start(f32[1,2,4,16,16,128]{5,4,3,2,1,0:T(8,128)} %pad_maximum_fusion.5) | copy-start | bytes 3145732
  31.3 2.9 %copy-start.6 = (f32[1,2,4,12,16,128]{5,3,4,2,1,0:T(8,128)S(1)}, f32[1,2,4,12,16,128]{5,3,4,2,1,0:T(8,128)}, u32[]{:S(2)}) copy-start(f32[1,2,4,12,16,128]{5,3,4,2,1,0:T(8,128)} %get-tuple-element.55) | copy-start | bytes 2359300
  31.3 3.0 %copy-start.7 = (f32[1,2,4,12,16,128]{5,3,4,2,1,0:T(8,128)S(1)}, f32[1,2,4,12,16,128]{5,3,4,2,1,0:T(8,128)}, u32[]{:S(2)}) copy-start(f32[1,2,4,12,16,128]{5,3,4,2,1,0:T(8,128)} %get-tuple-element.56) | copy-start | bytes 2359300
  31.3 3.0 %copy-start.8 = (f32[1,2,4,13,16,128]{5,3,4,2,1,0:T(8,128)S(1)}, f32[1,2,4,13,16,128]{5,3,4,2,1,0:T(8,128)}, u32[]{:S(2)}) copy-start(f32[1,2,4,13,16,128]{5,3,4,2,1,0:T(8,128)} %get-tuple-element.59) | copy-start | bytes 2555908
  31.3 3.0 %copy-start.9 = (f32[1,2,4,4,16,128]{5,3,4,2,1,0:T(4,128)S(1)}, f32[1,2,4,4,16,128]{5,3,4,2,1,0:T(4,128)}, u32[]{:S(2)}) copy-start(f32[1,2,4,4,16,128]{5,3,4,2,1,0:T(4,128)} %get-tuple-element.57) | copy-start | bytes 786436
  31.3 3.0 %copy-start.10 = (f32[1,2,4,4,16,128]{5,3,4,2,1,0:T(4,128)S(1)}, f32[1,2,4,4,16,128]{5,3,4,2,1,0:T(4,128)}, u32[]{:S(2)}) copy-start(f32[1,2,4,4,16,128]{5,3,4,2,1,0:T(4,128)} %get-tuple-element.58) | copy-start | bytes 786436
  31.3 3.0 %copy-start.13 = (f32[1,2,4,1,16,128]{5,3,4,2,1,0:T(1,128)S(1)}, f32[1,2,4,1,16,128]{5,3,4,2,1,0:T(1,128)}, u32[]{:S(2)}) copy-start(f32[1,2,4,1,16,128]{5,3,4,2,1,0:T(1,128)} %get-tuple-element.69) | copy-start | bytes 196612
  49.6 21.9 %collective-permute-start.4 = (f32[1,2,4,16,4,128]{5,3,4,2,1,0:T(8,128)}, f32[1,2,4,16,4,128]{5,3,4,2,1,0:T(8,128)S(1)}, u32[]{:S(2)}, u32[]{:S(2)}) collective-permute-start(f32[1,2,4,16,4,128]{5,3,4,2,1,0:T(8,128)} %get-tuple-element.53), channel_id=1, source_target_pairs={{4,0},{8,4},{12,8},{16,12},{20,16},{24,20},{28,24},{0,28},{5,1},{9... | collective-permute-start | bytes 786440 | tf_op jit(solution)/shard_map/ppermute | solution.py:24
  51.1 20.4 %collective-permute-start.5 = (f32[1,2,4,16,4,128]{5,3,4,2,1,0:T(8,128)}, f32[1,2,4,16,4,128]{5,3,4,2,1,0:T(8,128)}, u32[]{:S(2)}, u32[]{:S(2)}) collective-permute-start(f32[1,2,4,16,4,128]{5,3,4,2,1,0:T(8,128)} %get-tuple-element.54), channel_id=1, source_target_pairs={{0,4},{4,8},{8,12},{12,16},{16,20},{20,24},{24,28},{28,0},{1,5},{5... | collective-permute-start | bytes 786440 | tf_op jit(solution)/shard_map/ppermute | solution.py:23
  55.0 7.0 %collective-permute-start.6 = (f32[1,2,4,16,16,4]{4,3,5,2,1,0:T(8,128)}, f32[1,2,4,16,16,4]{4,3,5,2,1,0:T(8,128)}, u32[]{:S(2)}, u32[]{:S(2)}) collective-permute-start(f32[1,2,4,16,16,4]{4,3,5,2,1,0:T(8,128)} %copy.176), channel_id=1, source_target_pairs={{1,0},{2,1},{3,2},{0,3},{5,4},{6,5},{7,6},{4,7},{9,8},{10,9},{11,1... | collective-permute-start | bytes 98312 | tf_op jit(solution)/shard_map/ppermute | solution.py:24
  59.9 8.7 %collective-permute-start.7 = (f32[1,2,4,16,16,4]{4,3,5,2,1,0:T(8,128)}, f32[1,2,4,16,16,4]{4,3,5,2,1,0:T(8,128)}, u32[]{:S(2)}, u32[]{:S(2)}) collective-permute-start(f32[1,2,4,16,16,4]{4,3,5,2,1,0:T(8,128)} %copy.178), channel_id=1, source_target_pairs={{0,1},{1,2},{2,3},{3,0},{4,5},{5,6},{6,7},{7,4},{8,9},{9,10},{10,1... | collective-permute-start | bytes 98312 | tf_op jit(solution)/shard_map/ppermute | solution.py:23
  71.5 2.9 %copy-start.2 = (f32[1,2,4,12,16,128]{5,3,4,2,1,0:T(8,128)S(1)}, f32[1,2,4,12,16,128]{5,3,4,2,1,0:T(8,128)}, u32[]{:S(2)}) copy-start(f32[1,2,4,12,16,128]{5,3,4,2,1,0:T(8,128)} %get-tuple-element.35) | copy-start | bytes 2359300
  71.5 2.9 %copy-start.3 = (f32[1,2,4,12,16,128]{5,3,4,2,1,0:T(8,128)S(1)}, f32[1,2,4,12,16,128]{5,3,4,2,1,0:T(8,128)}, u32[]{:S(2)}) copy-start(f32[1,2,4,12,16,128]{5,3,4,2,1,0:T(8,128)} %get-tuple-element.36) | copy-start | bytes 2359300
  71.5 2.9 %copy-start.4 = (f32[1,2,4,13,16,128]{5,3,4,2,1,0:T(8,128)S(1)}, f32[1,2,4,13,16,128]{5,3,4,2,1,0:T(8,128)}, u32[]{:S(2)}) copy-start(f32[1,2,4,13,16,128]{5,3,4,2,1,0:T(8,128)} %get-tuple-element.39) | copy-start | bytes 2555908
  71.5 3.0 %copy-start.11 = (f32[1,2,4,4,16,128]{5,3,4,2,1,0:T(4,128)S(1)}, f32[1,2,4,4,16,128]{5,3,4,2,1,0:T(4,128)}, u32[]{:S(2)}) copy-start(f32[1,2,4,4,16,128]{5,3,4,2,1,0:T(4,128)} %get-tuple-element.37) | copy-start | bytes 786436
  71.5 3.0 %copy-start.12 = (f32[1,2,4,4,16,128]{5,3,4,2,1,0:T(4,128)S(1)}, f32[1,2,4,4,16,128]{5,3,4,2,1,0:T(4,128)}, u32[]{:S(2)}) copy-start(f32[1,2,4,4,16,128]{5,3,4,2,1,0:T(4,128)} %get-tuple-element.38) | copy-start | bytes 786436
  71.5 3.0 %copy-start.14 = (f32[1,2,4,1,16,128]{5,3,4,2,1,0:T(1,128)S(1)}, f32[1,2,4,1,16,128]{5,3,4,2,1,0:T(1,128)}, u32[]{:S(2)}) copy-start(f32[1,2,4,1,16,128]{5,3,4,2,1,0:T(1,128)} %get-tuple-element.49) | copy-start | bytes 196612
  79.4 19.1 %copy-start.18 = (f32[8]{0:T(128)S(1)}, f32[8]{0:T(128)}, u32[]{:S(2)}) copy-start(f32[8]{0:T(128)} %get-tuple-element.88) | copy-start | bytes 100
  79.4 19.1 %copy-start.19 = (f32[8]{0:T(128)S(1)}, f32[8]{0:T(128)}, u32[]{:S(2)}) copy-start(f32[8]{0:T(128)} %get-tuple-element.89) | copy-start | bytes 100
  79.4 19.3 %copy-start.15 = (f32[4,2,16,128]{3,2,1,0:T(8,128)S(1)}, f32[4,2,16,128]{3,2,1,0:T(8,128)}, u32[]{:S(2)}) copy-start(f32[4,2,16,128]{3,2,1,0:T(8,128)} %get-tuple-element.77) | copy-start | bytes 196612
  79.4 19.3 %copy-start.16 = (f32[4,2,16,128]{3,2,1,0:T(8,128)S(1)}, f32[4,2,16,128]{3,2,1,0:T(8,128)}, u32[]{:S(2)}) copy-start(f32[4,2,16,128]{3,2,1,0:T(8,128)} %get-tuple-element.78) | copy-start | bytes 196612
  81.0 17.2 %all-to-all-start = ((f32[32,1,32]{2,1,0:T(1,128)}), f32[32,1,32]{2,1,0:T(1,128)S(1)}, u32[]{:S(2)}, u32[]{:S(2)}) async-start(f32[32,1,32]{2,1,0:T(1,128)} %broadcast_in_dim.5), calls=%async_computation | async-start | bytes 32768 | tf_op jit(solution)/shard_map/all_to_all | solution.py:37

commit v2 on v1

v2 whole, which is shorter than its diff:
```python
import functools
import math

import jax
import jax.numpy as jnp
import numpy as np
from jax import lax
from jax.experimental import pallas as pl
from jax.experimental.pallas import tpu as pltpu
from jax.sharding import PartitionSpec as P

QPTS = 8
MOMS = 4
MESH = pl.DeviceIdType.MESH
LANES = 128
REACH = 4
stencil_weights = (-205.0 / 72.0, 8.0 / 5.0, -1.0 / 5.0, 8.0 / 315.0, -1.0 / 560.0)
half_weights = tuple(-0.5 * w for w in stencil_weights)


def complex_mul(left, right):
    return (left[0] * right[0] - left[1] * right[1], left[0] * right[1] + left[1] * right[0])


def complex_div(left, right):
    norm_sq = right[0] * right[0] + right[1] * right[1]
    return (
        (left[0] * right[0] + left[1] * right[1]) / norm_sq,
        (left[1] * right[0] - left[0] * right[1]) / norm_sq,
    )


def complex_sub(left, right):
    return (left[0] - right[0], left[1] - right[1])


def recip(value):
    norm_sq = value[0] * value[0] + value[1] * value[1]
    return (value[0] / norm_sq, -value[1] / norm_sq)


def coefficients(totals, shift):
    mu0, mu1, mu2, mu3 = totals
    tau = complex_div(mu1, mu0)
    tau_mu1 = complex_mul(tau, mu1)
    nu2 = complex_sub(mu2, tau_mu1)
    tau_mu2 = complex_mul(tau, mu2)
    nu3 = complex_sub(complex_sub(mu3, tau_mu2), complex_mul(tau, complex_sub(mu2, tau_mu1)))
    ratio = complex_div(nu3, nu2)
    slope = complex_div(nu2, mu0)
    alpha_first = recip(complex_sub(shift, tau))
    gamma = complex_mul(alpha_first, slope)
    alpha_next = recip(complex_sub(complex_sub(shift, ratio), gamma))
    image_part = complex_mul(alpha_first, alpha_next)
    back = complex_mul(image_part, complex_sub(gamma, tau))
    return (alpha_first[0] + back[0], alpha_first[1] + back[1]), image_part


def tables():
    theta = 2.0 * math.pi * (np.arange(QPTS) + 0.5) / QPTS
    rows = [np.cos(theta), np.sin(theta)]
    for k in range(1, MOMS + 1):
        rows += [np.cos(k * theta) / QPTS, np.sin(k * theta) / QPTS]
    return np.broadcast_to(np.stack(rows)[:, :, None], (2 + 2 * MOMS, QPTS, LANES)).astype(np.float32)


def neighbours(ny, nz, nquad):
    quad, py, pz = lax.axis_index("quad"), lax.axis_index("py"), lax.axis_index("pz")
    parts = 2
    deep = (quad % parts) * nz + pz

    def in_group(dy, dz):
        return (quad, (py + dy + ny) % ny, (pz + dz + nz) % nz)

    def along_z(dz):
        at = (deep + dz + parts * nz) % (parts * nz)
        return (quad - quad % parts + at // nz, py, at % nz)

    return in_group, along_z


def group_offsets(ny, nz):
    every = [(a, b) for a in range(-ny // 2 + 1, ny // 2 + 1) for b in range(-nz // 2 + 1, nz // 2 + 1)]
    every = [o for o in every if o != (0, 0)]
    return sorted(every, key=lambda o: -(abs(o[0]) + 2 * abs(o[1])))


def kernel(
    ny, nz, nquad, sr, si, pot, center, radius, points, out,
    field, image, poten, table, packed, left, right, joint, packed_image, left_image,
    partial, received, moments,
    load_sem, ysend, yrecv, zsend, zrecv, y2send, y2recv, z2send, z2recv, asend, arecv,
):
    nsrc, cx, ry, _ = sr.shape
    slab = cx // nquad
    top = 8
    own = pl.ds(top, ry)
    low_halo, high_halo = pl.ds(top - REACH, REACH), pl.ds(top + ry, REACH)
    low_rows, high_rows = pl.ds(top, REACH), pl.ds(top + ry - REACH, REACH)
    in_group, along_z = neighbours(ny, nz, nquad)
    offsets = group_offsets(ny, nz)

    loads = []
    for s in range(nsrc):
        for c, ref in enumerate((sr, si)):
            copy = pltpu.make_async_copy(ref.at[s], field.at[s, c, :, own, :], load_sem.at[2 * s + c])
            copy.start()
            loads.append(copy)
    load_pot = pltpu.make_async_copy(pot, poten, load_sem.at[2 * nsrc])
    load_pot.start()
    load_table = pltpu.make_async_copy(points, table, load_sem.at[2 * nsrc + 1])
    load_table.start()

    barrier = pltpu.get_barrier_semaphore()
    for dz in (-1, 1):
        pl.semaphore_signal(barrier, inc=1, device_id=along_z(dz), device_id_type=MESH)
    for dy, dz in offsets[::-1]:
        pl.semaphore_signal(barrier, inc=1, device_id=in_group(dy, dz), device_id_type=MESH)

    lane = lax.broadcasted_iota(jnp.int32, (ry, LANES), 1)

    def pack(buf, s, to):
        for c in range(2):
            total = jnp.zeros((ry, LANES), jnp.float32)
            for x in range(cx):
                moved = pltpu.roll(buf[s, c, x, own, :], 8 * x + REACH, 1)
                total = jnp.where(lane // 8 == x, moved, total)
            to[s, c] = total

    for copy in loads:
        copy.wait()
    for s in range(nsrc):
        pack(field, s, packed)
    pl.semaphore_wait(barrier, len(offsets) + 2)

    for s in range(nsrc):
        pltpu.make_async_remote_copy(
            field.at[s, :, :, high_rows, :], field.at[s, :, :, low_halo, :],
            ysend.at[0], yrecv.at[2 * s], device_id=in_group(1, 0), device_id_type=MESH,
        ).start()
        pltpu.make_async_remote_copy(
            field.at[s, :, :, low_rows, :], field.at[s, :, :, high_halo, :],
            ysend.at[1], yrecv.at[2 * s + 1], device_id=in_group(-1, 0), device_id_type=MESH,
        ).start()
        pltpu.make_async_remote_copy(
            packed.at[s], left.at[s], zsend.at[0], zrecv.at[2 * s],
            device_id=along_z(1), device_id_type=MESH,
        ).start()
        pltpu.make_async_remote_copy(
            packed.at[s], right.at[s], zsend.at[1], zrecv.at[2 * s + 1],
            device_id=along_z(-1), device_id_type=MESH,
        ).start()

    load_pot.wait()
    load_table.wait()
    diagonal = 3.0 * half_weights[0] - center[0]
    zero = jnp.zeros((8, LANES), jnp.float32)

    def halves(value):
        total = value[0:8]
        for at in range(8, ry, 8):
            total = total + value[at : at + 8]
        return total

    def add_forms(sums, u, v):
        re = halves(u[0] * v[0] - u[1] * v[1])
        im = halves(u[0] * v[1] + u[1] * v[0])
        return (sums[0] + re, sums[1] + im)

    def keep(sums, quantity, s):
        partial[quantity, s] = sums

    def image_of(s):
        def step(x, sums):
            first, second, third = sums
            both = []
            for c in range(2):
                f = field[s, c, x, own, :]
                edge = pltpu.roll(joint[s, c], (LANES - REACH + (cx - x) * 8) % LANES, 1)
                total = (poten[x] + diagonal) * f
                for k in range(1, REACH + 1):
                    beside = field[s, c, (x + k) % cx, own, :] + field[s, c, (x + cx - k) % cx, own, :]
                    beside = beside + field[s, c, x, pl.ds(top - k, ry), :]
                    beside = beside + field[s, c, x, pl.ds(top + k, ry), :]
                    beside = beside + pltpu.roll(jnp.where(lane >= LANES - k, edge, f), k, 1)
                    beside = beside + pltpu.roll(jnp.where(lane < k, edge, f), LANES - k, 1)
                    total = total + half_weights[k] * beside
                image[s, c, x, own, :] = total
                both.append((f, total))
            u = (both[0][0], both[1][0])
            w = (both[0][1], both[1][1])
            return (add_forms(first, u, u), add_forms(second, u, w), add_forms(third, w, w))

        sums = lax.fori_loop(0, cx, step, ((zero, zero),) * 3, unroll=2)
        for i in range(3):
            for c in range(2):
                keep(sums[i][c], 2 * i + c, s)

    def last_form(s):
        sign = -1 if s < nsrc // 2 else 1

        def step(x, sums):
            w, once = [], []
            for c in range(2):
                f = image[s, c, x, own, :]
                edge = pltpu.roll(left_image[s, c], (LANES - REACH + (cx - x) * 8) % LANES, 1)
                total = (poten[x] + diagonal) * f
                for k in range(1, REACH + 1):
                    beside = image[s, c, (x + cx - k) % cx, own, :]
                    beside = beside + image[s, c, x, pl.ds(top + sign * k, ry), :]
                    beside = beside + pltpu.roll(jnp.where(lane >= LANES - k, edge, f), k, 1)
                    total = total + 2.0 * half_weights[k] * beside
                w.append(f)
                once.append(total)
            return add_forms(sums, w, once)

        sums = lax.fori_loop(0, cx, step, (zero, zero), unroll=2)
        for c in range(2):
            keep(sums[c], 6 + c, s)

    wide = field.at[0, :, :, low_halo, :]
    for s in range(nsrc):
        for sem in (yrecv.at[2 * s], yrecv.at[2 * s + 1]):
            pltpu.make_async_copy(wide, wide, sem).wait()
        for sem in (zrecv.at[2 * s], zrecv.at[2 * s + 1]):
            pltpu.make_async_copy(left.at[s], left.at[s], sem).wait()
        for c in range(2):
            joint[s, c] = jnp.where(lane % 8 < REACH, left[s, c], right[s, c])
        image_of(s)
        pack(image, s, packed_image)
        if s < nsrc // 2:
            pltpu.make_async_remote_copy(
                image.at[s, :, :, high_rows, :], image.at[s, :, :, low_halo, :],
                y2send, y2recv.at[s], device_id=in_group(1, 0), device_id_type=MESH,
            ).start()
        else:
            pltpu.make_async_remote_copy(
                image.at[s, :, :, low_rows, :], image.at[s, :, :, high_halo, :],
                y2send, y2recv.at[s], device_id=in_group(-1, 0), device_id_type=MESH,
            ).start()
        pltpu.make_async_remote_copy(
            packed_image.at[s], left_image.at[s], z2send, z2recv.at[s],
            device_id=along_z(1), device_id_type=MESH,
        ).start()

    spot = lax.broadcasted_iota(jnp.int32, (1, LANES), 1) // (LANES // (8 * nsrc))

    def gather_sums(quantities, row):
        for q in quantities:
            for s in range(nsrc):
                total = jnp.sum(partial[q, s], axis=0, keepdims=True)
                total = jnp.sum(total, axis=1, keepdims=True)
                row = jnp.where(spot == q * nsrc + s, total, row)
        return row

    row = gather_sums(range(6), jnp.zeros((1, LANES), jnp.float32))
    for s in range(nsrc):
        pltpu.make_async_copy(wide, wide, y2recv.at[s]).wait()
        pltpu.make_async_copy(left.at[s], left.at[s], z2recv.at[s]).wait()
        last_form(s)
    moments[...] = gather_sums(range(6, 8), row)

    for j, (dy, dz) in enumerate(offsets):
        pltpu.make_async_remote_copy(
            moments, received.at[j], asend, arecv, device_id=in_group(dy, dz), device_id_type=MESH,
        ).start()
    pltpu.make_async_copy(received, received, arecv).wait()
    total = moments[...]
    for j in range(len(offsets)):
        total = total + received[j]

    wide_total = jnp.broadcast_to(total, (QPTS, LANES))
    lanes_each = LANES // 8
    forms = [
        wide_total if q == 0 else pltpu.roll(wide_total, LANES - q * lanes_each, 1) for q in range(8)
    ]
    reach = radius[0]
    shift = (reach * table[0], reach * table[1])
    parts = coefficients([(forms[2 * i], forms[2 * i + 1]) for i in range(4)], shift)
    weights = {}
    for k in range(MOMS):
        factor = (reach * table[2 + 2 * k], reach * table[3 + 2 * k])
        for i, part in enumerate(parts):
            both = complex_mul(factor, part)
            for c in range(2):
                weights[k, i, c] = jnp.sum(both[c], axis=0, keepdims=True)

    first = lax.axis_index("quad") * slab
    write_output(out, field, image, weights, first, slab, own, nsrc)

    for i, halo in enumerate((low_halo, high_halo)):
        every = field.at[:, :, :, halo, :]
        pltpu.make_async_copy(every, every, ysend.at[i]).wait()
        pltpu.make_async_copy(packed, packed, zsend.at[i]).wait()
    every = image.at[:, :, :, low_halo, :]
    pltpu.make_async_copy(every, every, y2send).wait()
    pltpu.make_async_copy(packed_image, packed_image, z2send).wait()
    pltpu.make_async_copy(received, received, asend).wait()


def write_output(out, field, image, weights, first, slab, own, nsrc):
    for s in range(nsrc):
        lane_at = s * (LANES // (8 * nsrc))
        for k in range(MOMS):
            a = [weights[k, 0, c][:, lane_at : lane_at + 1] for c in range(2)]
            d = [weights[k, 1, c][:, lane_at : lane_at + 1] for c in range(2)]
            for x in range(slab):
                b = [field[s, c, first + x, own, :] for c in range(2)]
                w = [image[s, c, first + x, own, :] for c in range(2)]
                out[k, 0, s, x] = a[0] * b[0] - a[1] * b[1] + d[0] * w[0] - d[1] * w[1]
                out[k, 1, s, x] = a[0] * b[1] + a[1] * b[0] + d[0] * w[1] + d[1] * w[0]


def solution(mesh):
    nquad, ny, nz = mesh.shape["quad"], mesh.shape["py"], mesh.shape["pz"]

    def per_device(source_real, source_imag, potential, center, radius):
        nsrc, cx, ry, width = source_real.shape
        vmem, smem, hbm = pltpu.VMEM, pltpu.SMEM, pltpu.HBM
        padded = (nsrc, 2, cx, ry + 16, width)
        strips = (nsrc, 2, ry, width)
        peers = ny * nz - 1
        dma = pltpu.SemaphoreType.DMA
        f32 = jnp.float32

        def in_hbm(value):
            return pltpu.with_memory_space_constraint(value, hbm)

        return pl.pallas_call(
            functools.partial(kernel, ny, nz, nquad),
            out_shape=jax.ShapeDtypeStruct((MOMS, 2, nsrc, cx // nquad, ry, width), f32),
            in_specs=[
                pl.BlockSpec(memory_space=hbm),
                pl.BlockSpec(memory_space=hbm),
                pl.BlockSpec(memory_space=hbm),
                pl.BlockSpec(memory_space=smem),
                pl.BlockSpec(memory_space=smem),
                pl.BlockSpec(memory_space=hbm),
            ],
            out_specs=pl.BlockSpec(memory_space=vmem),
            scratch_shapes=[
                vmem(padded, f32), vmem(padded, f32), vmem((cx, ry, width), f32),
                vmem((2 + 2 * MOMS, QPTS, width), f32),
                vmem(strips, f32), vmem(strips, f32), vmem(strips, f32), vmem(strips, f32),
                vmem(strips, f32), vmem(strips, f32),
                vmem((8, nsrc, 8, width), f32), vmem((peers, 1, width), f32), vmem((1, width), f32),
                dma((2 * nsrc + 2,)), dma((2,)), dma((2 * nsrc,)), dma((2,)), dma((2 * nsrc,)),
                dma, dma((nsrc,)), dma, dma((nsrc,)), dma, dma,
            ],
            compiler_params=pltpu.CompilerParams(
                collective_id=0, has_side_effects=True, vmem_limit_bytes=32 * 1024 * 1024
            ),
        )(
            in_hbm(source_real), in_hbm(source_imag), in_hbm(potential), center, radius,
            in_hbm(jnp.asarray(tables())),
        )

    in_specs = (P(None, None, "py", "pz"), P(None, None, "py", "pz"), P(None, "py", "pz"), P(), P())
    out_specs = P(None, None, None, "quad", "py", "pz")
    return jax.shard_map(
        per_device, mesh=mesh, in_specs=in_specs, out_specs=out_specs, check_vma=False
    )
```

time: 100 us -> 34.1 us (0.34)
  local copies, waits for them, and re-layouts: 41.2 us -> 0.8 us
  Pallas kernels: 0 us -> 31.9 us
  starting transfers between devices: 22.2 us -> 0 us
  other arithmetic: 21.4 us -> 0 us
  waiting for transfers between devices: 13.2 us -> 0 us
    pallas_call x0 -> x1, Pallas kernels: none -> 31.9 us  [per_device(): pl.pallas_call(functools.partial(kernel, ny, nz, nquad), out_shape=jax.Sh...]
    slice x24 -> x0, local copies, waits for them, and re-layouts: 30.2 us -> none  [the longest x16 19 us: apply_operator(): beside_all = jnp.roll(field, offset, 3) + jnp.roll(field, -offset, 3)]
    ppermute x8 -> x0, starting transfers between devices: 12.1 us -> none  [the longest x4 11.9 us: with_halo(): lax.ppermute(initial, axis, [(b, a) for a, b in up])]
    add x5 -> x0, other arithmetic: 10.3 us -> none  [the longest x2 9.9 us: apply_operator(): return -0.5 * laplace + potential * field]
    all_to_all x1 -> x0, starting transfers between devices: 10 us -> none  [sent_to_all(): lax.all_to_all(jnp.broadcast_to(value[None], (count, *value.shape)), axis...]
    ppermute x4 -> x0, local copies, waits for them, and re-layouts: 9.13 us -> none  [the longest x2 5.59 us: with_halo(): lax.ppermute(last, axis, up)]
    all_to_all x1 -> x0, waiting for transfers between devices: 7.04 us -> none  [sent_to_all(): lax.all_to_all(jnp.broadcast_to(value[None], (count, *value.shape)), axis...]
    ppermute x8 -> x0, waiting for transfers between devices: 6.2 us -> none  [the longest x4 4.88 us: with_halo(): lax.ppermute(last, axis, up)]
  transfers between devices with their start and end apart: 9 -> 0, of which waited for: 3 -> 0; matrix products, arithmetic and copies ran while one was open for 31% -> 0% of each run, Pallas kernels for 0% -> 0%
where the time goes in v2:
time: 34.1 us; the launch traced here: 34 us
  Pallas kernels  31.9 us (94%)
  between operations  1.3 us (4%)
  local copies, waits for them, and re-layouts  0.8 us (2%)
    pallas_call x1, Pallas kernels, per_device(): pl.pallas_call(functools.partial(kernel, ny, nz, nquad), out_shape=jax.Sh...  31.9 us
    unnamed x1, local copies, waits for them, and re-layouts  0.8 us

profile of v2, /device:TPU:1, one launch (start us, length us, event | category | flops | bytes accessed | tf_op | source)
XLA Modules:
  0.0 34.0 jit_solution(1348577975912648567)
XLA Ops:
  1.3 31.9 %shard_map.64 = f32[4,2,4,2,16,128]{5,4,3,2,1,0:T(8,128)S(1)} custom-call(f32[4,16,16,128]{3,2,1,0:T(8,128)} %sr.1, f32[4,16,16,128]{3,2,1,0:T(8,128)} %si.1, f32[16,16,128]{2,1,0:T(8,128)} %pot.1, f32[1]{0:T(128)S(6)} %copy.8.center, f32[1]{0:T(128)S(6)} %copy.9.radius, f32[10,8,128]{2,1,0:T(8,128)} %constant.2.clone.points), custom_call_target="tpu_custom_call" | custom-call | tf_op jit(solution)/shard_map/pallas_call | solution.py:329
  33.2 0.8 %copy.10 = f32[4,2,4,2,16,128]{5,4,3,2,1,0:T(8,128)} copy(f32[4,2,4,2,16,128]{5,4,3,2,1,0:T(8,128)S(1)} %shard_map.64) | data formatting | bytes 1048576

commit v3 on v2

--- a/solution.py
+++ b/solution.py
@@ -85,20 +85,36 @@
     return sorted(every, key=lambda o: -(abs(o[0]) + 2 * abs(o[1])))
 
 
+def band(shape, one_sided):
+    at = lax.broadcasted_iota(jnp.int32, shape, 0) % LANES
+    to = lax.broadcasted_iota(jnp.int32, shape, 1)
+    ahead = to % LANES - at
+    value = jnp.zeros(shape, jnp.float32)
+    for k in range(1, REACH + 1):
+        hit = ahead == k if one_sided else jnp.abs(ahead) == k
+        value = jnp.where(hit, (2.0 if one_sided else 1.0) * half_weights[k], value)
+    high = value.astype(jnp.bfloat16)
+    low = (value - high.astype(jnp.float32)).astype(jnp.bfloat16)
+    return jnp.where(to < LANES, high.astype(jnp.float32), low.astype(jnp.float32)).astype(jnp.bfloat16)
+
+
 def kernel(
     ny, nz, nquad, sr, si, pot, center, radius, points, out,
-    field, image, poten, table, packed, left, right, joint, packed_image, left_image,
-    partial, received, moments,
+    field, image, halo, halo2, poten, table, packed, left, right, packed_image, left_image,
+    split, zpart, two_sided, one_sided, partial, received, moments,
     load_sem, ysend, yrecv, zsend, zrecv, y2send, y2recv, z2send, z2recv, asend, arecv,
 ):
     nsrc, cx, ry, _ = sr.shape
     slab = cx // nquad
+    half = cx // 2
+    group = 4
     top = 8
     own = pl.ds(top, ry)
     low_halo, high_halo = pl.ds(top - REACH, REACH), pl.ds(top + ry, REACH)
     low_rows, high_rows = pl.ds(top, REACH), pl.ds(top + ry - REACH, REACH)
     in_group, along_z = neighbours(ny, nz, nquad)
     offsets = group_offsets(ny, nz)
+    first_half, second_half = pl.ds(0, half), pl.ds(half, half)
 
     loads = []
     for s in range(nsrc):
@@ -118,8 +134,40 @@
         pl.semaphore_signal(barrier, inc=1, device_id=in_group(dy, dz), device_id_type=MESH)
 
     lane = lax.broadcasted_iota(jnp.int32, (ry, LANES), 1)
-
-    def pack(buf, s, to):
+    zero_tile = jnp.zeros((top, LANES), jnp.float32)
+    zero = jnp.zeros((8, LANES), jnp.float32)
+
+    def clear(i, carry):
+        s = i // cx
+        x = i % cx
+        for c in range(2):
+            for buf in (field, image):
+                buf[s, c, x, pl.ds(0, top), :] = zero_tile
+                buf[s, c, x, pl.ds(top + ry, top), :] = zero_tile
+            for buf in (halo, halo2):
+                for at in range(0, ry, top):
+                    buf[s, c, x, pl.ds(top + at, top), :] = zero_tile
+        return carry
+
+    lax.fori_loop(0, nsrc * cx, clear, 0, unroll=2)
+    two_sided[...] = band(two_sided.shape, False)
+    one_sided[...] = band(one_sided.shape, True)
+
+    for copy in loads:
+        copy.wait()
+    pl.semaphore_wait(barrier, len(offsets) + 2)
+
+    for s in range(nsrc):
+        pltpu.make_async_remote_copy(
+            field.at[s, :, :, high_rows, :], halo.at[s, :, :, low_halo, :],
+            ysend.at[0], yrecv.at[2 * s], device_id=in_group(1, 0), device_id_type=MESH,
+        ).start()
+        pltpu.make_async_remote_copy(
+            field.at[s, :, :, low_rows, :], halo.at[s, :, :, high_halo, :],
+            ysend.at[1], yrecv.at[2 * s + 1], device_id=in_group(-1, 0), device_id_type=MESH,
+        ).start()
+
+    def pack_into(buf, to, s):
         for c in range(2):
             total = jnp.zeros((ry, LANES), jnp.float32)
             for x in range(cx):
@@ -127,21 +175,8 @@
                 total = jnp.where(lane // 8 == x, moved, total)
             to[s, c] = total
 
-    for copy in loads:
-        copy.wait()
-    for s in range(nsrc):
-        pack(field, s, packed)
-    pl.semaphore_wait(barrier, len(offsets) + 2)
-
-    for s in range(nsrc):
-        pltpu.make_async_remote_copy(
-            field.at[s, :, :, high_rows, :], field.at[s, :, :, low_halo, :],
-            ysend.at[0], yrecv.at[2 * s], device_id=in_group(1, 0), device_id_type=MESH,
-        ).start()
-        pltpu.make_async_remote_copy(
-            field.at[s, :, :, low_rows, :], field.at[s, :, :, high_halo, :],
-            ysend.at[1], yrecv.at[2 * s + 1], device_id=in_group(-1, 0), device_id_type=MESH,
-        ).start()
+    def pack(s, carry):
+        pack_into(field, packed, s)
         pltpu.make_async_remote_copy(
             packed.at[s], left.at[s], zsend.at[0], zrecv.at[2 * s],
             device_id=along_z(1), device_id_type=MESH,
@@ -150,11 +185,13 @@
             packed.at[s], right.at[s], zsend.at[1], zrecv.at[2 * s + 1],
             device_id=along_z(-1), device_id_type=MESH,
         ).start()
+        return carry
+
+    lax.fori_loop(0, nsrc, pack, 0)
 
     load_pot.wait()
     load_table.wait()
     diagonal = 3.0 * half_weights[0] - center[0]
-    zero = jnp.zeros((8, LANES), jnp.float32)
 
     def halves(value):
         total = value[0:8]
@@ -167,81 +204,127 @@
         im = halves(u[0] * v[1] + u[1] * v[0])
         return (sums[0] + re, sums[1] + im)
 
-    def keep(sums, quantity, s):
-        partial[quantity, s] = sums
-
-    def image_of(s):
-        def step(x, sums):
-            first, second, third = sums
-            both = []
-            for c in range(2):
-                f = field[s, c, x, own, :]
-                edge = pltpu.roll(joint[s, c], (LANES - REACH + (cx - x) * 8) % LANES, 1)
-                total = (poten[x] + diagonal) * f
-                for k in range(1, REACH + 1):
-                    beside = field[s, c, (x + k) % cx, own, :] + field[s, c, (x + cx - k) % cx, own, :]
-                    beside = beside + field[s, c, x, pl.ds(top - k, ry), :]
-                    beside = beside + field[s, c, x, pl.ds(top + k, ry), :]
-                    beside = beside + pltpu.roll(jnp.where(lane >= LANES - k, edge, f), k, 1)
-                    beside = beside + pltpu.roll(jnp.where(lane < k, edge, f), LANES - k, 1)
-                    total = total + half_weights[k] * beside
-                image[s, c, x, own, :] = total
-                both.append((f, total))
-            u = (both[0][0], both[1][0])
-            w = (both[0][1], both[1][1])
-            return (add_forms(first, u, u), add_forms(second, u, w), add_forms(third, w, w))
-
-        sums = lax.fori_loop(0, cx, step, ((zero, zero),) * 3, unroll=2)
-        for i in range(3):
-            for c in range(2):
-                keep(sums[i][c], 2 * i + c, s)
-
-    def last_form(s):
-        sign = -1 if s < nsrc // 2 else 1
-
-        def step(x, sums):
-            w, once = [], []
+    def rows_of(c, x):
+        return pl.ds(pl.multiple_of((c * cx + x) * ry, ry), ry)
+
+    def put_split(c, x, value):
+        high = value.astype(jnp.bfloat16)
+        split[rows_of(c, x), 0:LANES] = high
+        split[rows_of(c, x), LANES : 2 * LANES] = (value - high.astype(jnp.float32)).astype(jnp.bfloat16)
+
+    def multiply(matrix):
+        zpart[...] = jnp.dot(split[...], matrix[...], preferred_element_type=jnp.float32)
+
+    def stage(buf, s):
+        def step(g, carry):
+            for i in range(group):
+                for c in range(2):
+                    put_split(c, g * group + i, buf[s, c, g * group + i, own, :])
+            return carry
+
+        lax.fori_loop(0, cx // group, step, 0)
+
+    def along_lanes(c, x):
+        return zpart[rows_of(c, x), 0:LANES] + zpart[rows_of(c, x), LANES : 2 * LANES]
+
+    def local_image(s, carry):
+        stage(field, s)
+        multiply(two_sided)
+
+        def step(g, carry):
+            for i in range(group):
+                x = g * group + i
+                scale = poten[x] + diagonal
+                for c in range(2):
+                    total = scale * field[s, c, x, own, :] + along_lanes(c, x)
+                    for k in range(1, REACH + 1):
+                        beside = field[s, c, (x + k) % cx, own, :] + field[s, c, (x + cx - k) % cx, own, :]
+                        beside = beside + field[s, c, x, pl.ds(top - k, ry), :]
+                        beside = beside + field[s, c, x, pl.ds(top + k, ry), :]
+                        total = total + half_weights[k] * beside
+                    image[s, c, x, own, :] = total
+            return carry
+
+        lax.fori_loop(0, cx // group, step, 0)
+        return carry
+
+    lax.fori_loop(0, nsrc, local_image, 0)
+
+    wide = field.at[0, :, :, low_halo, :]
+    narrow = field.at[0, :, first_half, low_halo, :]
+    tile_zero = jnp.zeros((ry, LANES), jnp.float32)
+    low_part = lane % 8 < REACH
+    at_edge = (lane < REACH) | (lane >= LANES - REACH)
+
+    def finish(s, carry):
+        for i in range(2):
+            pltpu.make_async_copy(wide, wide, yrecv.at[2 * s + i]).wait()
+            pltpu.make_async_copy(left.at[s], left.at[s], zrecv.at[2 * s + i]).wait()
+        edges = []
+        for c in range(2):
+            below = jnp.where(low_part, left[s, c], 0.0)
+            above = jnp.where(low_part, 0.0, right[s, c])
+            total = tile_zero
+            for k in range(1, REACH + 1):
+                near = pltpu.roll(below, k, 1) * jnp.where(low_part, 0.0, half_weights[k])
+                near = near + pltpu.roll(above, LANES - k, 1) * jnp.where(low_part, half_weights[k], 0.0)
+                total = total + near
+            edges.append(total)
+
+        for x in range(cx):
             for c in range(2):
                 f = image[s, c, x, own, :]
-                edge = pltpu.roll(left_image[s, c], (LANES - REACH + (cx - x) * 8) % LANES, 1)
-                total = (poten[x] + diagonal) * f
+                moved = pltpu.roll(edges[c], (2 * LANES - REACH - 8 * x) % LANES, 1)
+                down, up = zero, zero
                 for k in range(1, REACH + 1):
-                    beside = image[s, c, (x + cx - k) % cx, own, :]
-                    beside = beside + image[s, c, x, pl.ds(top + sign * k, ry), :]
-                    beside = beside + pltpu.roll(jnp.where(lane >= LANES - k, edge, f), k, 1)
-                    total = total + 2.0 * half_weights[k] * beside
-                w.append(f)
-                once.append(total)
-            return add_forms(sums, w, once)
-
-        sums = lax.fori_loop(0, cx, step, (zero, zero), unroll=2)
-        for c in range(2):
-            keep(sums[c], 6 + c, s)
-
-    wide = field.at[0, :, :, low_halo, :]
-    for s in range(nsrc):
-        for sem in (yrecv.at[2 * s], yrecv.at[2 * s + 1]):
-            pltpu.make_async_copy(wide, wide, sem).wait()
-        for sem in (zrecv.at[2 * s], zrecv.at[2 * s + 1]):
-            pltpu.make_async_copy(left.at[s], left.at[s], sem).wait()
-        for c in range(2):
-            joint[s, c] = jnp.where(lane % 8 < REACH, left[s, c], right[s, c])
-        image_of(s)
-        pack(image, s, packed_image)
-        if s < nsrc // 2:
-            pltpu.make_async_remote_copy(
-                image.at[s, :, :, high_rows, :], image.at[s, :, :, low_halo, :],
-                y2send, y2recv.at[s], device_id=in_group(1, 0), device_id_type=MESH,
-            ).start()
-        else:
-            pltpu.make_async_remote_copy(
-                image.at[s, :, :, low_rows, :], image.at[s, :, :, high_halo, :],
-                y2send, y2recv.at[s], device_id=in_group(-1, 0), device_id_type=MESH,
-            ).start()
+                    down = down + half_weights[k] * halo[s, c, x, pl.ds(top - k, top), :]
+                    up = up + half_weights[k] * halo[s, c, x, pl.ds(ry + k, top), :]
+                image[s, c, x, own, :] = f + jnp.concatenate([down, up], 0) + jnp.where(at_edge, moved, 0.0)
+
+        pltpu.make_async_remote_copy(
+            image.at[s, :, first_half, high_rows, :], halo2.at[s, :, first_half, low_halo, :],
+            y2send.at[0], y2recv.at[2 * s], device_id=in_group(1, 0), device_id_type=MESH,
+        ).start()
+        pltpu.make_async_remote_copy(
+            image.at[s, :, second_half, low_rows, :], halo2.at[s, :, second_half, high_halo, :],
+            y2send.at[1], y2recv.at[2 * s + 1], device_id=in_group(-1, 0), device_id_type=MESH,
+        ).start()
+        pack_into(image, packed_image, s)
         pltpu.make_async_remote_copy(
             packed_image.at[s], left_image.at[s], z2send, z2recv.at[s],
             device_id=along_z(1), device_id_type=MESH,
         ).start()
+
+        stage(image, s)
+        multiply(one_sided)
+        sums = ((zero, zero),) * 4
+        for upper in range(2):
+            def pairs(g, sums):
+                for i in range(group):
+                    x = upper * half + g * group + i
+                    scale = poten[x] + diagonal
+                    b, w, once = [], [], []
+                    for c in range(2):
+                        f = image[s, c, x, own, :]
+                        total = scale * f + along_lanes(c, x)
+                        b.append(field[s, c, x, own, :])
+                        for k in range(1, REACH + 1):
+                            beside = image[s, c, (x + cx - k) % cx, own, :]
+                            beside = beside + image[s, c, x, pl.ds(top + (k if upper else -k), ry), :]
+                            total = total + 2.0 * half_weights[k] * beside
+                        w.append(f)
+                        once.append(total)
+                    sides = ((b, b), (b, w), (w, w), (w, once))
+                    sums = tuple(add_forms(old, *pair) for old, pair in zip(sums, sides))
+                return sums
+
+            sums = lax.fori_loop(0, half // group, pairs, sums)
+        for i in range(4):
+            for c in range(2):
+                partial[2 * i + c, s] = sums[i][c]
+        return carry
+
+    lax.fori_loop(0, nsrc, finish, 0)
 
     spot = lax.broadcasted_iota(jnp.int32, (1, LANES), 1) // (LANES // (8 * nsrc))
 
@@ -254,10 +337,42 @@
         return row
 
     row = gather_sums(range(6), jnp.zeros((1, LANES), jnp.float32))
-    for s in range(nsrc):
-        pltpu.make_async_copy(wide, wide, y2recv.at[s]).wait()
+
+    def across(s, carry):
+        for i in range(2):
+            pltpu.make_async_copy(narrow, narrow, y2recv.at[2 * s + i]).wait()
         pltpu.make_async_copy(left.at[s], left.at[s], z2recv.at[s]).wait()
-        last_form(s)
+        once = []
+        for c in range(2):
+            below = jnp.where(low_part, left_image[s, c], 0.0)
+            total = tile_zero
+            for k in range(1, REACH + 1):
+                total = total + 2.0 * half_weights[k] * pltpu.roll(below, k, 1)
+            once.append(jnp.where(low_part, 0.0, total))
+        sums = add_forms((partial[6, s], partial[7, s]), (packed_image[s, 0], packed_image[s, 1]), once)
+        for upper in range(2):
+            def step(g, sums):
+                for i in range(group):
+                    x = upper * half + g * group + i
+                    w, once = [], []
+                    for c in range(2):
+                        total = zero
+                        for k in range(1, REACH + 1):
+                            at = ry + k if upper else top - k
+                            total = total + 2.0 * half_weights[k] * halo2[s, c, x, pl.ds(at, top), :]
+                        once.append(total)
+                        w.append(image[s, c, x, pl.ds(ry if upper else top, top), :])
+                    re = w[0] * once[0] - w[1] * once[1]
+                    im = w[0] * once[1] + w[1] * once[0]
+                    sums = (sums[0] + re, sums[1] + im)
+                return sums
+
+            sums = lax.fori_loop(0, half // group, step, sums)
+        for c in range(2):
+            partial[6 + c, s] = sums[c]
+        return carry
+
+    lax.fori_loop(0, nsrc, across, 0)
     moments[...] = gather_sums(range(6, 8), row)
 
     for j, (dy, dz) in enumerate(offsets):
@@ -288,12 +403,12 @@
     first = lax.axis_index("quad") * slab
     write_output(out, field, image, weights, first, slab, own, nsrc)
 
-    for i, halo in enumerate((low_halo, high_halo)):
-        every = field.at[:, :, :, halo, :]
+    for i, strip in enumerate((low_halo, high_halo)):
+        every = field.at[:, :, :, strip, :]
         pltpu.make_async_copy(every, every, ysend.at[i]).wait()
         pltpu.make_async_copy(packed, packed, zsend.at[i]).wait()
-    every = image.at[:, :, :, low_halo, :]
-    pltpu.make_async_copy(every, every, y2send).wait()
+        every = image.at[:, :, first_half, strip, :]
+        pltpu.make_async_copy(every, every, y2send.at[i]).wait()
     pltpu.make_async_copy(packed_image, packed_image, z2send).wait()
     pltpu.make_async_copy(received, received, asend).wait()
 
@@ -339,13 +454,14 @@
             ],
             out_specs=pl.BlockSpec(memory_space=vmem),
             scratch_shapes=[
-                vmem(padded, f32), vmem(padded, f32), vmem((cx, ry, width), f32),
-                vmem((2 + 2 * MOMS, QPTS, width), f32),
-                vmem(strips, f32), vmem(strips, f32), vmem(strips, f32), vmem(strips, f32),
-                vmem(strips, f32), vmem(strips, f32),
+                vmem(padded, f32), vmem(padded, f32), vmem(padded, f32), vmem(padded, f32),
+                vmem((cx, ry, width), f32), vmem((2 + 2 * MOMS, QPTS, width), f32),
+                vmem(strips, f32), vmem(strips, f32), vmem(strips, f32), vmem(strips, f32), vmem(strips, f32),
+                vmem((2 * cx * ry, 2 * width), jnp.bfloat16), vmem((2 * cx * ry, 2 * width), f32),
+                vmem((2 * width, 2 * width), jnp.bfloat16), vmem((2 * width, 2 * width), jnp.bfloat16),
                 vmem((8, nsrc, 8, width), f32), vmem((peers, 1, width), f32), vmem((1, width), f32),
                 dma((2 * nsrc + 2,)), dma((2,)), dma((2 * nsrc,)), dma((2,)), dma((2 * nsrc,)),
-                dma, dma((nsrc,)), dma, dma((nsrc,)), dma, dma,
+                dma((2,)), dma((2 * nsrc,)), dma, dma((nsrc,)), dma, dma,
             ],
             compiler_params=pltpu.CompilerParams(
                 collective_id=0, has_side_effects=True, vmem_limit_bytes=32 * 1024 * 1024

time: 34.1 us -> 27.6 us (0.81)
  Pallas kernels: 31.9 us -> 25.4 us
    pallas_call x1, Pallas kernels: 31.9 us -> 25.4 us  [per_device(): pl.pallas_call(functools.partial(kernel, ny, nz, nquad), out_shape=jax.Sh...]
where the time goes in v3:
time: 27.6 us; the launch traced here: 27.5 us
  Pallas kernels  25.4 us (92%)
  between operations  1.3 us (5%)
  local copies, waits for them, and re-layouts  0.8 us (3%)
    pallas_call x1, Pallas kernels, per_device(): pl.pallas_call(functools.partial(kernel, ny, nz, nquad), out_shape=jax.Sh...  25.4 us
    unnamed x1, local copies, waits for them, and re-layouts  0.8 us

profile of v3, /device:TPU:1, one launch (start us, length us, event | category | flops | bytes accessed | tf_op | source)
XLA Modules:
  0.0 27.5 jit_solution(9484312822893134210)
XLA Ops:
  1.3 25.4 %shard_map.64 = f32[4,2,4,2,16,128]{5,4,3,2,1,0:T(8,128)S(1)} custom-call(f32[4,16,16,128]{3,2,1,0:T(8,128)} %sr.1, f32[4,16,16,128]{3,2,1,0:T(8,128)} %si.1, f32[16,16,128]{2,1,0:T(8,128)} %pot.1, f32[1]{0:T(128)S(6)} %copy.8.center, f32[1]{0:T(128)S(6)} %copy.9.radius, f32[10,8,128]{2,1,0:T(8,128)} %constant.2.clone.points), custom_call_target="tpu_custom_call" | custom-call | tf_op jit(solution)/shard_map/pallas_call | solution.py:444
  26.7 0.8 %copy.10 = f32[4,2,4,2,16,128]{5,4,3,2,1,0:T(8,128)} copy(f32[4,2,4,2,16,128]{5,4,3,2,1,0:T(8,128)S(1)} %shard_map.64) | data formatting | bytes 1048576

commit v4 on v3

--- a/solution.py
+++ b/solution.py
@@ -64,6 +64,10 @@
     return np.broadcast_to(np.stack(rows)[:, :, None], (2 + 2 * MOMS, QPTS, LANES)).astype(np.float32)
 
 
+BESIDE = ((1, 0), (-1, 0), (0, 1), (0, -1))
+RELAY = (BESIDE, ((2, 0), (-2, 0), (0, 2), (0, -2)), ((4, 0), (0, 3), (0, -3)))
+
+
 def neighbours(ny, nz, nquad):
     quad, py, pz = lax.axis_index("quad"), lax.axis_index("py"), lax.axis_index("pz")
     parts = 2
@@ -72,11 +76,11 @@
     def in_group(dy, dz):
         return (quad, (py + dy + ny) % ny, (pz + dz + nz) % nz)
 
-    def along_z(dz):
+    def along(dy, dz):
         at = (deep + dz + parts * nz) % (parts * nz)
-        return (quad - quad % parts + at // nz, py, at % nz)
-
-    return in_group, along_z
+        return (quad - quad % parts + at // nz, (py + dy + ny) % ny, at % nz)
+
+    return in_group, along
 
 
 def group_offsets(ny, nz):
@@ -102,7 +106,7 @@
     ny, nz, nquad, sr, si, pot, center, radius, points, out,
     field, image, halo, halo2, poten, table, packed, left, right, packed_image, left_image,
     split, zpart, two_sided, one_sided, partial, received, moments,
-    load_sem, ysend, yrecv, zsend, zrecv, y2send, y2recv, z2send, z2recv, asend, arecv,
+    load_sem, ysend, yrecv, zsend, zrecv, y2send, y2recv, z2send, z2recv, asend, arecv, entered,
 ):
     nsrc, cx, ry, _ = sr.shape
     slab = cx // nquad
@@ -112,7 +116,7 @@
     own = pl.ds(top, ry)
     low_halo, high_halo = pl.ds(top - REACH, REACH), pl.ds(top + ry, REACH)
     low_rows, high_rows = pl.ds(top, REACH), pl.ds(top + ry - REACH, REACH)
-    in_group, along_z = neighbours(ny, nz, nquad)
+    in_group, along = neighbours(ny, nz, nquad)
     offsets = group_offsets(ny, nz)
     first_half, second_half = pl.ds(0, half), pl.ds(half, half)
 
@@ -128,10 +132,17 @@
     load_table.start()
 
     barrier = pltpu.get_barrier_semaphore()
-    for dz in (-1, 1):
-        pl.semaphore_signal(barrier, inc=1, device_id=along_z(dz), device_id_type=MESH)
-    for dy, dz in offsets[::-1]:
-        pl.semaphore_signal(barrier, inc=1, device_id=in_group(dy, dz), device_id_type=MESH)
+    for dy, dz in BESIDE:
+        pl.semaphore_signal(barrier, inc=1, device_id=along(dy, dz), device_id_type=MESH)
+
+    def pass_on(stage_at):
+        for dy, dz in RELAY[stage_at]:
+            pl.semaphore_signal(
+                entered.at[stage_at], inc=1, device_id=along(dy, dz), device_id_type=MESH
+            )
+
+    def hear(stage_at):
+        pl.semaphore_wait(entered.at[stage_at], len(RELAY[stage_at]))
 
     lane = lax.broadcasted_iota(jnp.int32, (ry, LANES), 1)
     zero_tile = jnp.zeros((top, LANES), jnp.float32)
@@ -155,7 +166,7 @@
 
     for copy in loads:
         copy.wait()
-    pl.semaphore_wait(barrier, len(offsets) + 2)
+    pl.semaphore_wait(barrier, len(BESIDE))
 
     for s in range(nsrc):
         pltpu.make_async_remote_copy(
@@ -179,15 +190,16 @@
         pack_into(field, packed, s)
         pltpu.make_async_remote_copy(
             packed.at[s], left.at[s], zsend.at[0], zrecv.at[2 * s],
-            device_id=along_z(1), device_id_type=MESH,
+            device_id=along(0, 1), device_id_type=MESH,
         ).start()
         pltpu.make_async_remote_copy(
             packed.at[s], right.at[s], zsend.at[1], zrecv.at[2 * s + 1],
-            device_id=along_z(-1), device_id_type=MESH,
+            device_id=along(0, -1), device_id_type=MESH,
         ).start()
         return carry
 
     lax.fori_loop(0, nsrc, pack, 0)
+    pass_on(0)
 
     load_pot.wait()
     load_table.wait()
@@ -249,6 +261,8 @@
         return carry
 
     lax.fori_loop(0, nsrc, local_image, 0)
+    hear(0)
+    pass_on(1)
 
     wide = field.at[0, :, :, low_halo, :]
     narrow = field.at[0, :, first_half, low_halo, :]
@@ -292,7 +306,7 @@
         pack_into(image, packed_image, s)
         pltpu.make_async_remote_copy(
             packed_image.at[s], left_image.at[s], z2send, z2recv.at[s],
-            device_id=along_z(1), device_id_type=MESH,
+            device_id=along(0, 1), device_id_type=MESH,
         ).start()
 
         stage(image, s)
@@ -325,6 +339,8 @@
         return carry
 
     lax.fori_loop(0, nsrc, finish, 0)
+    hear(1)
+    pass_on(2)
 
     spot = lax.broadcasted_iota(jnp.int32, (1, LANES), 1) // (LANES // (8 * nsrc))
 
@@ -374,6 +390,7 @@
 
     lax.fori_loop(0, nsrc, across, 0)
     moments[...] = gather_sums(range(6, 8), row)
+    hear(2)
 
     for j, (dy, dz) in enumerate(offsets):
         pltpu.make_async_remote_copy(
@@ -462,6 +479,7 @@
                 vmem((8, nsrc, 8, width), f32), vmem((peers, 1, width), f32), vmem((1, width), f32),
                 dma((2 * nsrc + 2,)), dma((2,)), dma((2 * nsrc,)), dma((2,)), dma((2 * nsrc,)),
                 dma((2,)), dma((2 * nsrc,)), dma, dma((nsrc,)), dma, dma,
+                pltpu.SemaphoreType.REGULAR((len(RELAY),)),
             ],
             compiler_params=pltpu.CompilerParams(
                 collective_id=0, has_side_effects=True, vmem_limit_bytes=32 * 1024 * 1024

time: 27.6 us -> 25.5 us (0.924)
  Pallas kernels: 25.4 us -> 23.2 us
    pallas_call x1, Pallas kernels: 25.4 us -> 23.2 us  [per_device(): pl.pallas_call(functools.partial(kernel, ny, nz, nquad), out_shape=jax.Sh...]
where the time goes in v4:
time: 25.5 us; the launch traced here: 25.3 us
  Pallas kernels  23.2 us (91%)
  between operations  1.3 us (5%)
  local copies, waits for them, and re-layouts  0.8 us (3%)
    pallas_call x1, Pallas kernels, per_device(): pl.pallas_call(functools.partial(kernel, ny, nz, nquad), out_shape=jax.Sh...  23.2 us
    unnamed x1, local copies, waits for them, and re-layouts  0.8 us

profile of v4, /device:TPU:1, one launch (start us, length us, event | category | flops | bytes accessed | tf_op | source)
XLA Modules:
  0.0 25.3 jit_solution(17592052777741302488)
XLA Ops:
  1.3 23.2 %shard_map.64 = f32[4,2,4,2,16,128]{5,4,3,2,1,0:T(8,128)S(1)} custom-call(f32[4,16,16,128]{3,2,1,0:T(8,128)} %sr.1, f32[4,16,16,128]{3,2,1,0:T(8,128)} %si.1, f32[16,16,128]{2,1,0:T(8,128)} %pot.1, f32[1]{0:T(128)S(6)} %copy.8.center, f32[1]{0:T(128)S(6)} %copy.9.radius, f32[10,8,128]{2,1,0:T(8,128)} %constant.2.clone.points), custom_call_target="tpu_custom_call" | custom-call | tf_op jit(solution)/shard_map/pallas_call | solution.py:461
  24.5 0.8 %copy.10 = f32[4,2,4,2,16,128]{5,4,3,2,1,0:T(8,128)} copy(f32[4,2,4,2,16,128]{5,4,3,2,1,0:T(8,128)S(1)} %shard_map.64) | data formatting | bytes 1048576

commit v5 on v4

--- a/solution.py
+++ b/solution.py
@@ -65,22 +65,7 @@
 
 
 BESIDE = ((1, 0), (-1, 0), (0, 1), (0, -1))
-RELAY = (BESIDE, ((2, 0), (-2, 0), (0, 2), (0, -2)), ((4, 0), (0, 3), (0, -3)))
-
-
-def neighbours(ny, nz, nquad):
-    quad, py, pz = lax.axis_index("quad"), lax.axis_index("py"), lax.axis_index("pz")
-    parts = 2
-    deep = (quad % parts) * nz + pz
-
-    def in_group(dy, dz):
-        return (quad, (py + dy + ny) % ny, (pz + dz + nz) % nz)
-
-    def along(dy, dz):
-        at = (deep + dz + parts * nz) % (parts * nz)
-        return (quad - quad % parts + at // nz, (py + dy + ny) % ny, at % nz)
-
-    return in_group, along
+RELAY = (BESIDE, ((2, 0), (-2, 0), (0, 2)), ((4, 0),))
 
 
 def group_offsets(ny, nz):
@@ -104,7 +89,7 @@
 
 def kernel(
     ny, nz, nquad, sr, si, pot, center, radius, points, out,
-    field, image, halo, halo2, poten, table, packed, left, right, packed_image, left_image,
+    field, image, halo, halo2, poten, table, up, down, left, right, image_strip, image_up, left_image,
     split, zpart, two_sided, one_sided, partial, received, moments,
     load_sem, ysend, yrecv, zsend, zrecv, y2send, y2recv, z2send, z2recv, asend, arecv, entered,
 ):
@@ -116,7 +101,11 @@
     own = pl.ds(top, ry)
     low_halo, high_halo = pl.ds(top - REACH, REACH), pl.ds(top + ry, REACH)
     low_rows, high_rows = pl.ds(top, REACH), pl.ds(top + ry - REACH, REACH)
-    in_group, along = neighbours(ny, nz, nquad)
+    quad, py, pz = lax.axis_index("quad"), lax.axis_index("py"), lax.axis_index("pz")
+
+    def in_group(dy, dz):
+        return (quad, (py + dy + ny) % ny, (pz + dz + nz) % nz)
+
     offsets = group_offsets(ny, nz)
     first_half, second_half = pl.ds(0, half), pl.ds(half, half)
 
@@ -133,12 +122,12 @@
 
     barrier = pltpu.get_barrier_semaphore()
     for dy, dz in BESIDE:
-        pl.semaphore_signal(barrier, inc=1, device_id=along(dy, dz), device_id_type=MESH)
+        pl.semaphore_signal(barrier, inc=1, device_id=in_group(dy, dz), device_id_type=MESH)
 
     def pass_on(stage_at):
         for dy, dz in RELAY[stage_at]:
             pl.semaphore_signal(
-                entered.at[stage_at], inc=1, device_id=along(dy, dz), device_id_type=MESH
+                entered.at[stage_at], inc=1, device_id=in_group(dy, dz), device_id_type=MESH
             )
 
     def hear(stage_at):
@@ -166,39 +155,52 @@
 
     for copy in loads:
         copy.wait()
-    pl.semaphore_wait(barrier, len(BESIDE))
-
-    for s in range(nsrc):
-        pltpu.make_async_remote_copy(
-            field.at[s, :, :, high_rows, :], halo.at[s, :, :, low_halo, :],
-            ysend.at[0], yrecv.at[2 * s], device_id=in_group(1, 0), device_id_type=MESH,
-        ).start()
-        pltpu.make_async_remote_copy(
-            field.at[s, :, :, low_rows, :], halo.at[s, :, :, high_halo, :],
-            ysend.at[1], yrecv.at[2 * s + 1], device_id=in_group(-1, 0), device_id_type=MESH,
-        ).start()
-
-    def pack_into(buf, to, s):
+    low_part = lane % 8 < REACH
+
+    def strips_of(buf, s):
+        parts = []
         for c in range(2):
             total = jnp.zeros((ry, LANES), jnp.float32)
             for x in range(cx):
                 moved = pltpu.roll(buf[s, c, x, own, :], 8 * x + REACH, 1)
                 total = jnp.where(lane // 8 == x, moved, total)
-            to[s, c] = total
+            parts.append(total)
+        return parts
+
+    def last_lanes(parts):
+        return jnp.where(low_part, parts[0], pltpu.roll(parts[1], REACH, 1))
+
+    def from_last(both):
+        return [jnp.where(low_part, t, 0.0) for t in (both, pltpu.roll(both, LANES - REACH, 1))]
 
     def pack(s, carry):
-        pack_into(field, packed, s)
-        pltpu.make_async_remote_copy(
-            packed.at[s], left.at[s], zsend.at[0], zrecv.at[2 * s],
-            device_id=along(0, 1), device_id_type=MESH,
-        ).start()
-        pltpu.make_async_remote_copy(
-            packed.at[s], right.at[s], zsend.at[1], zrecv.at[2 * s + 1],
-            device_id=along(0, -1), device_id_type=MESH,
-        ).start()
+        parts = strips_of(field, s)
+        up[s] = last_lanes(parts)
+        down[s] = jnp.where(low_part, pltpu.roll(parts[0], LANES - REACH, 1), parts[1])
         return carry
 
     lax.fori_loop(0, nsrc, pack, 0)
+    pl.semaphore_wait(barrier, len(BESIDE))
+
+    for s in range(nsrc):
+        pltpu.make_async_remote_copy(
+            up.at[s], left.at[s], zsend.at[0], zrecv.at[2 * s],
+            device_id=in_group(0, 1), device_id_type=MESH,
+        ).start()
+        pltpu.make_async_remote_copy(
+            down.at[s], right.at[s], zsend.at[1], zrecv.at[2 * s + 1],
+            device_id=in_group(0, -1), device_id_type=MESH,
+        ).start()
+
+    for s in range(nsrc):
+        pltpu.make_async_remote_copy(
+            field.at[s, :, :, high_rows, :], halo.at[s, :, :, low_halo, :],
+            ysend.at[0], yrecv.at[2 * s], device_id=in_group(1, 0), device_id_type=MESH,
+        ).start()
+        pltpu.make_async_remote_copy(
+            field.at[s, :, :, low_rows, :], halo.at[s, :, :, high_halo, :],
+            ysend.at[1], yrecv.at[2 * s + 1], device_id=in_group(-1, 0), device_id_type=MESH,
+        ).start()
     pass_on(0)
 
     load_pot.wait()
@@ -267,7 +269,6 @@
     wide = field.at[0, :, :, low_halo, :]
     narrow = field.at[0, :, first_half, low_halo, :]
     tile_zero = jnp.zeros((ry, LANES), jnp.float32)
-    low_part = lane % 8 < REACH
     at_edge = (lane < REACH) | (lane >= LANES - REACH)
 
     def finish(s, carry):
@@ -275,9 +276,9 @@
             pltpu.make_async_copy(wide, wide, yrecv.at[2 * s + i]).wait()
             pltpu.make_async_copy(left.at[s], left.at[s], zrecv.at[2 * s + i]).wait()
         edges = []
-        for c in range(2):
-            below = jnp.where(low_part, left[s, c], 0.0)
-            above = jnp.where(low_part, 0.0, right[s, c])
+        belows = from_last(left[s])
+        aboves = [jnp.where(low_part, 0.0, t) for t in (pltpu.roll(right[s], REACH, 1), right[s])]
+        for below, above in zip(belows, aboves):
             total = tile_zero
             for k in range(1, REACH + 1):
                 near = pltpu.roll(below, k, 1) * jnp.where(low_part, 0.0, half_weights[k])
@@ -303,12 +304,21 @@
             image.at[s, :, second_half, low_rows, :], halo2.at[s, :, second_half, high_halo, :],
             y2send.at[1], y2recv.at[2 * s + 1], device_id=in_group(-1, 0), device_id_type=MESH,
         ).start()
-        pack_into(image, packed_image, s)
-        pltpu.make_async_remote_copy(
-            packed_image.at[s], left_image.at[s], z2send, z2recv.at[s],
-            device_id=along(0, 1), device_id_type=MESH,
-        ).start()
-
+        parts = strips_of(image, s)
+        for c in range(2):
+            image_strip[s, c] = parts[c]
+        image_up[s] = last_lanes(parts)
+        pltpu.make_async_remote_copy(
+            image_up.at[s], left_image.at[s], z2send, z2recv.at[s],
+            device_id=in_group(0, 1), device_id_type=MESH,
+        ).start()
+        return carry
+
+    lax.fori_loop(0, nsrc, finish, 0)
+    hear(1)
+    pass_on(2)
+
+    def inner(s, carry):
         stage(image, s)
         multiply(one_sided)
         sums = ((zero, zero),) * 4
@@ -338,9 +348,7 @@
                 partial[2 * i + c, s] = sums[i][c]
         return carry
 
-    lax.fori_loop(0, nsrc, finish, 0)
-    hear(1)
-    pass_on(2)
+    lax.fori_loop(0, nsrc, inner, 0)
 
     spot = lax.broadcasted_iota(jnp.int32, (1, LANES), 1) // (LANES // (8 * nsrc))
 
@@ -359,13 +367,12 @@
             pltpu.make_async_copy(narrow, narrow, y2recv.at[2 * s + i]).wait()
         pltpu.make_async_copy(left.at[s], left.at[s], z2recv.at[s]).wait()
         once = []
-        for c in range(2):
-            below = jnp.where(low_part, left_image[s, c], 0.0)
+        for below in from_last(left_image[s]):
             total = tile_zero
             for k in range(1, REACH + 1):
                 total = total + 2.0 * half_weights[k] * pltpu.roll(below, k, 1)
             once.append(jnp.where(low_part, 0.0, total))
-        sums = add_forms((partial[6, s], partial[7, s]), (packed_image[s, 0], packed_image[s, 1]), once)
+        sums = add_forms((partial[6, s], partial[7, s]), (image_strip[s, 0], image_strip[s, 1]), once)
         for upper in range(2):
             def step(g, sums):
                 for i in range(group):
@@ -423,10 +430,10 @@
     for i, strip in enumerate((low_halo, high_halo)):
         every = field.at[:, :, :, strip, :]
         pltpu.make_async_copy(every, every, ysend.at[i]).wait()
-        pltpu.make_async_copy(packed, packed, zsend.at[i]).wait()
+        pltpu.make_async_copy(up, up, zsend.at[i]).wait()
         every = image.at[:, :, first_half, strip, :]
         pltpu.make_async_copy(every, every, y2send.at[i]).wait()
-    pltpu.make_async_copy(packed_image, packed_image, z2send).wait()
+    pltpu.make_async_copy(image_up, image_up, z2send).wait()
     pltpu.make_async_copy(received, received, asend).wait()
 
 
@@ -450,7 +457,7 @@
         nsrc, cx, ry, width = source_real.shape
         vmem, smem, hbm = pltpu.VMEM, pltpu.SMEM, pltpu.HBM
         padded = (nsrc, 2, cx, ry + 16, width)
-        strips = (nsrc, 2, ry, width)
+        strips = (nsrc, ry, width)
         peers = ny * nz - 1
         dma = pltpu.SemaphoreType.DMA
         f32 = jnp.float32
@@ -473,7 +480,8 @@
             scratch_shapes=[
                 vmem(padded, f32), vmem(padded, f32), vmem(padded, f32), vmem(padded, f32),
                 vmem((cx, ry, width), f32), vmem((2 + 2 * MOMS, QPTS, width), f32),
-                vmem(strips, f32), vmem(strips, f32), vmem(strips, f32), vmem(strips, f32), vmem(strips, f32),
+                vmem(strips, f32), vmem(strips, f32), vmem(strips, f32), vmem(strips, f32),
+                vmem((nsrc, 2, ry, width), f32), vmem(strips, f32), vmem(strips, f32),
                 vmem((2 * cx * ry, 2 * width), jnp.bfloat16), vmem((2 * cx * ry, 2 * width), f32),
                 vmem((2 * width, 2 * width), jnp.bfloat16), vmem((2 * width, 2 * width), jnp.bfloat16),
                 vmem((8, nsrc, 8, width), f32), vmem((peers, 1, width), f32), vmem((1, width), f32),

time: 25.5 us -> 24.1 us (0.945)
  Pallas kernels: 23.2 us -> 21.9 us
    pallas_call x1, Pallas kernels: 23.2 us -> 21.9 us  [per_device(): pl.pallas_call(functools.partial(kernel, ny, nz, nquad), out_shape=jax.Sh...]
where the time goes in v5:
time: 24.1 us; the launch traced here: 24 us
  Pallas kernels  21.9 us (91%)
  between operations  1.3 us (5%)
  local copies, waits for them, and re-layouts  0.8 us (3%)
    pallas_call x1, Pallas kernels, per_device(): pl.pallas_call(functools.partial(kernel, ny, nz, nquad), out_shape=jax.Sh...  21.9 us
    unnamed x1, local copies, waits for them, and re-layouts  0.8 us

profile of v5, /device:TPU:1, one launch (start us, length us, event | category | flops | bytes accessed | tf_op | source)
XLA Modules:
  0.0 24.0 jit_solution(9668696987284541172)
XLA Ops:
  1.3 21.9 %shard_map.64 = f32[4,2,4,2,16,128]{5,4,3,2,1,0:T(8,128)S(1)} custom-call(f32[4,16,16,128]{3,2,1,0:T(8,128)} %sr.1, f32[4,16,16,128]{3,2,1,0:T(8,128)} %si.1, f32[16,16,128]{2,1,0:T(8,128)} %pot.1, f32[1]{0:T(128)S(6)} %copy.8.center, f32[1]{0:T(128)S(6)} %copy.9.radius, f32[10,8,128]{2,1,0:T(8,128)} %constant.2.clone.points), custom_call_target="tpu_custom_call" | custom-call | tf_op jit(solution)/shard_map/pallas_call | solution.py:468
  23.2 0.8 %copy.10 = f32[4,2,4,2,16,128]{5,4,3,2,1,0:T(8,128)} copy(f32[4,2,4,2,16,128]{5,4,3,2,1,0:T(8,128)S(1)} %shard_map.64) | data formatting | bytes 1048576

commit v6 on v5

--- a/solution.py
+++ b/solution.py
@@ -74,14 +74,13 @@
     return sorted(every, key=lambda o: -(abs(o[0]) + 2 * abs(o[1])))
 
 
-def band(shape, one_sided):
+def band(shape):
     at = lax.broadcasted_iota(jnp.int32, shape, 0) % LANES
     to = lax.broadcasted_iota(jnp.int32, shape, 1)
     ahead = to % LANES - at
     value = jnp.zeros(shape, jnp.float32)
     for k in range(1, REACH + 1):
-        hit = ahead == k if one_sided else jnp.abs(ahead) == k
-        value = jnp.where(hit, (2.0 if one_sided else 1.0) * half_weights[k], value)
+        value = jnp.where(jnp.abs(ahead) == k, half_weights[k], value)
     high = value.astype(jnp.bfloat16)
     low = (value - high.astype(jnp.float32)).astype(jnp.bfloat16)
     return jnp.where(to < LANES, high.astype(jnp.float32), low.astype(jnp.float32)).astype(jnp.bfloat16)
@@ -90,7 +89,7 @@
 def kernel(
     ny, nz, nquad, sr, si, pot, center, radius, points, out,
     field, image, halo, halo2, poten, table, up, down, left, right, image_strip, image_up, left_image,
-    split, zpart, two_sided, one_sided, partial, received, moments,
+    split, zpart, two_sided, partial, received, moments,
     load_sem, ysend, yrecv, zsend, zrecv, y2send, y2recv, z2send, z2recv, asend, arecv, entered,
 ):
     nsrc, cx, ry, _ = sr.shape
@@ -150,8 +149,7 @@
         return carry
 
     lax.fori_loop(0, nsrc * cx, clear, 0, unroll=2)
-    two_sided[...] = band(two_sided.shape, False)
-    one_sided[...] = band(one_sided.shape, True)
+    two_sided[...] = band(two_sided.shape)
 
     for copy in loads:
         copy.wait()
@@ -218,13 +216,13 @@
         im = halves(u[0] * v[1] + u[1] * v[0])
         return (sums[0] + re, sums[1] + im)
 
-    def rows_of(c, x):
-        return pl.ds(pl.multiple_of((c * cx + x) * ry, ry), ry)
-
-    def put_split(c, x, value):
+    def rows_of(s, c, x):
+        return pl.ds(pl.multiple_of(((s * 2 + c) * cx + x) * ry, ry), ry)
+
+    def put_split(s, c, x, value):
         high = value.astype(jnp.bfloat16)
-        split[rows_of(c, x), 0:LANES] = high
-        split[rows_of(c, x), LANES : 2 * LANES] = (value - high.astype(jnp.float32)).astype(jnp.bfloat16)
+        split[rows_of(s, c, x), 0:LANES] = high
+        split[rows_of(s, c, x), LANES : 2 * LANES] = (value - high.astype(jnp.float32)).astype(jnp.bfloat16)
 
     def multiply(matrix):
         zpart[...] = jnp.dot(split[...], matrix[...], preferred_element_type=jnp.float32)
@@ -233,26 +231,27 @@
         def step(g, carry):
             for i in range(group):
                 for c in range(2):
-                    put_split(c, g * group + i, buf[s, c, g * group + i, own, :])
+                    put_split(s, c, g * group + i, buf[s, c, g * group + i, own, :])
             return carry
 
         lax.fori_loop(0, cx // group, step, 0)
 
-    def along_lanes(c, x):
-        return zpart[rows_of(c, x), 0:LANES] + zpart[rows_of(c, x), LANES : 2 * LANES]
+    def along_lanes(s, c, x):
+        return zpart[rows_of(s, c, x), 0:LANES] + zpart[rows_of(s, c, x), LANES : 2 * LANES]
 
     def local_image(s, carry):
-        stage(field, s)
-        multiply(two_sided)
-
         def step(g, carry):
+            layers = [
+                [field[s, c, (g * group + (cx + d)) % cx, own, :] for d in range(-REACH, group + REACH)]
+                for c in range(2)
+            ]
             for i in range(group):
                 x = g * group + i
                 scale = poten[x] + diagonal
                 for c in range(2):
-                    total = scale * field[s, c, x, own, :] + along_lanes(c, x)
+                    total = scale * layers[c][i + REACH] + along_lanes(s, c, x)
                     for k in range(1, REACH + 1):
-                        beside = field[s, c, (x + k) % cx, own, :] + field[s, c, (x + cx - k) % cx, own, :]
+                        beside = layers[c][i + REACH + k] + layers[c][i + REACH - k]
                         beside = beside + field[s, c, x, pl.ds(top - k, ry), :]
                         beside = beside + field[s, c, x, pl.ds(top + k, ry), :]
                         total = total + half_weights[k] * beside
@@ -262,6 +261,12 @@
         lax.fori_loop(0, cx // group, step, 0)
         return carry
 
+    def stage_field(s, carry):
+        stage(field, s)
+        return carry
+
+    lax.fori_loop(0, nsrc, stage_field, 0)
+    multiply(two_sided)
     lax.fori_loop(0, nsrc, local_image, 0)
     hear(0)
     pass_on(1)
@@ -318,9 +323,9 @@
     hear(1)
     pass_on(2)
 
+    inside = [jnp.where(lane >= k, 2.0 * half_weights[k], 0.0) for k in range(1, REACH + 1)]
+
     def inner(s, carry):
-        stage(image, s)
-        multiply(one_sided)
         sums = ((zero, zero),) * 4
         for upper in range(2):
             def pairs(g, sums):
@@ -330,12 +335,13 @@
                     b, w, once = [], [], []
                     for c in range(2):
                         f = image[s, c, x, own, :]
-                        total = scale * f + along_lanes(c, x)
+                        total = scale * f
                         b.append(field[s, c, x, own, :])
                         for k in range(1, REACH + 1):
                             beside = image[s, c, (x + cx - k) % cx, own, :]
                             beside = beside + image[s, c, x, pl.ds(top + (k if upper else -k), ry), :]
                             total = total + 2.0 * half_weights[k] * beside
+                            total = total + inside[k - 1] * pltpu.roll(f, k, 1)
                         w.append(f)
                         once.append(total)
                     sides = ((b, b), (b, w), (w, w), (w, once))
@@ -373,24 +379,23 @@
                 total = total + 2.0 * half_weights[k] * pltpu.roll(below, k, 1)
             once.append(jnp.where(low_part, 0.0, total))
         sums = add_forms((partial[6, s], partial[7, s]), (image_strip[s, 0], image_strip[s, 1]), once)
-        for upper in range(2):
-            def step(g, sums):
-                for i in range(group):
-                    x = upper * half + g * group + i
-                    w, once = [], []
-                    for c in range(2):
-                        total = zero
-                        for k in range(1, REACH + 1):
-                            at = ry + k if upper else top - k
-                            total = total + 2.0 * half_weights[k] * halo2[s, c, x, pl.ds(at, top), :]
-                        once.append(total)
-                        w.append(image[s, c, x, pl.ds(ry if upper else top, top), :])
-                    re = w[0] * once[0] - w[1] * once[1]
-                    im = w[0] * once[1] + w[1] * once[0]
-                    sums = (sums[0] + re, sums[1] + im)
-                return sums
-
-            sums = lax.fori_loop(0, half // group, step, sums)
+        found = [[sums], []]
+        for x in range(cx):
+            upper = x >= half
+            w, once = [], []
+            for c in range(2):
+                total = zero
+                for k in range(1, REACH + 1):
+                    at = ry + k if upper else top - k
+                    total = total + 2.0 * half_weights[k] * halo2[s, c, x, pl.ds(at, top), :]
+                once.append(total)
+                w.append(image[s, c, x, pl.ds(ry if upper else top, top), :])
+            found[x % 2].append(complex_mul(w, once))
+        totals = []
+        for c in range(2):
+            both = [sum((f[c] for f in side[1:]), side[0][c]) for side in found]
+            totals.append(both[0] + both[1])
+        sums = tuple(totals)
         for c in range(2):
             partial[6 + c, s] = sums[c]
         return carry
@@ -404,9 +409,10 @@
             moments, received.at[j], asend, arecv, device_id=in_group(dy, dz), device_id_type=MESH,
         ).start()
     pltpu.make_async_copy(received, received, arecv).wait()
-    total = moments[...]
-    for j in range(len(offsets)):
-        total = total + received[j]
+    chains = [moments[...]] + [received[j] for j in range(3)]
+    for j in range(3, len(offsets)):
+        chains[j % 4] = chains[j % 4] + received[j]
+    total = (chains[0] + chains[1]) + (chains[2] + chains[3])
 
     wide_total = jnp.broadcast_to(total, (QPTS, LANES))
     lanes_each = LANES // 8
@@ -482,8 +488,8 @@
                 vmem((cx, ry, width), f32), vmem((2 + 2 * MOMS, QPTS, width), f32),
                 vmem(strips, f32), vmem(strips, f32), vmem(strips, f32), vmem(strips, f32),
                 vmem((nsrc, 2, ry, width), f32), vmem(strips, f32), vmem(strips, f32),
-                vmem((2 * cx * ry, 2 * width), jnp.bfloat16), vmem((2 * cx * ry, 2 * width), f32),
-                vmem((2 * width, 2 * width), jnp.bfloat16), vmem((2 * width, 2 * width), jnp.bfloat16),
+                vmem((2 * nsrc * cx * ry, 2 * width), jnp.bfloat16), vmem((2 * nsrc * cx * ry, 2 * width), f32),
+                vmem((2 * width, 2 * width), jnp.bfloat16),
                 vmem((8, nsrc, 8, width), f32), vmem((peers, 1, width), f32), vmem((1, width), f32),
                 dma((2 * nsrc + 2,)), dma((2,)), dma((2 * nsrc,)), dma((2,)), dma((2 * nsrc,)),
                 dma((2,)), dma((2 * nsrc,)), dma, dma((nsrc,)), dma, dma,

time: 24.1 us -> 23.5 us (0.975)
  Pallas kernels: 21.9 us -> 21.3 us
    pallas_call x1, Pallas kernels: 21.9 us -> 21.3 us  [per_device(): pl.pallas_call(functools.partial(kernel, ny, nz, nquad), out_shape=jax.Sh...]
where the time goes in v6:
time: 23.5 us; the launch traced here: 23.4 us
  Pallas kernels  21.3 us (91%)
  between operations  1.3 us (6%)
  local copies, waits for them, and re-layouts  0.8 us (3%)
    pallas_call x1, Pallas kernels, per_device(): pl.pallas_call(functools.partial(kernel, ny, nz, nquad), out_shape=jax.Sh...  21.3 us
    unnamed x1, local copies, waits for them, and re-layouts  0.8 us

profile of v6, /device:TPU:1, one launch (start us, length us, event | category | flops | bytes accessed | tf_op | source)
XLA Modules:
  0.0 23.4 jit_solution(7338868288196247577)
XLA Ops:
  1.3 21.3 %shard_map.64 = f32[4,2,4,2,16,128]{5,4,3,2,1,0:T(8,128)S(1)} custom-call(f32[4,16,16,128]{3,2,1,0:T(8,128)} %sr.1, f32[4,16,16,128]{3,2,1,0:T(8,128)} %si.1, f32[16,16,128]{2,1,0:T(8,128)} %pot.1, f32[1]{0:T(128)S(6)} %copy.8.center, f32[1]{0:T(128)S(6)} %copy.9.radius, f32[10,8,128]{2,1,0:T(8,128)} %constant.2.clone.points), custom_call_target="tpu_custom_call" | custom-call | tf_op jit(solution)/shard_map/pallas_call | solution.py:474
  22.6 0.8 %copy.10 = f32[4,2,4,2,16,128]{5,4,3,2,1,0:T(8,128)} copy(f32[4,2,4,2,16,128]{5,4,3,2,1,0:T(8,128)S(1)} %shard_map.64) | data formatting | bytes 1048576

commit v7 on v6

--- a/solution.py
+++ b/solution.py
@@ -108,6 +108,10 @@
     offsets = group_offsets(ny, nz)
     first_half, second_half = pl.ds(0, half), pl.ds(half, half)
 
+    barrier = pltpu.get_barrier_semaphore()
+    for dy, dz in BESIDE[::-1]:
+        pl.semaphore_signal(barrier, inc=1, device_id=in_group(dy, dz), device_id_type=MESH)
+
     loads = []
     for s in range(nsrc):
         for c, ref in enumerate((sr, si)):
@@ -119,10 +123,6 @@
     load_table = pltpu.make_async_copy(points, table, load_sem.at[2 * nsrc + 1])
     load_table.start()
 
-    barrier = pltpu.get_barrier_semaphore()
-    for dy, dz in BESIDE:
-        pl.semaphore_signal(barrier, inc=1, device_id=in_group(dy, dz), device_id_type=MESH)
-
     def pass_on(stage_at):
         for dy, dz in RELAY[stage_at]:
             pl.semaphore_signal(
@@ -151,8 +151,6 @@
     lax.fori_loop(0, nsrc * cx, clear, 0, unroll=2)
     two_sided[...] = band(two_sided.shape)
 
-    for copy in loads:
-        copy.wait()
     low_part = lane % 8 < REACH
 
     def strips_of(buf, s):
@@ -177,8 +175,21 @@
         down[s] = jnp.where(low_part, pltpu.roll(parts[0], LANES - REACH, 1), parts[1])
         return carry
 
-    lax.fori_loop(0, nsrc, pack, 0)
+    for s in range(nsrc):
+        loads[2 * s].wait()
+        loads[2 * s + 1].wait()
+        pack(s, 0)
     pl.semaphore_wait(barrier, len(BESIDE))
+
+    for s in range(nsrc):
+        pltpu.make_async_remote_copy(
+            field.at[s, :, :, high_rows, :], halo.at[s, :, :, low_halo, :],
+            ysend.at[0], yrecv.at[2 * s], device_id=in_group(1, 0), device_id_type=MESH,
+        ).start()
+        pltpu.make_async_remote_copy(
+            field.at[s, :, :, low_rows, :], halo.at[s, :, :, high_halo, :],
+            ysend.at[1], yrecv.at[2 * s + 1], device_id=in_group(-1, 0), device_id_type=MESH,
+        ).start()
 
     for s in range(nsrc):
         pltpu.make_async_remote_copy(
@@ -188,16 +199,6 @@
         pltpu.make_async_remote_copy(
             down.at[s], right.at[s], zsend.at[1], zrecv.at[2 * s + 1],
             device_id=in_group(0, -1), device_id_type=MESH,
-        ).start()
-
-    for s in range(nsrc):
-        pltpu.make_async_remote_copy(
-            field.at[s, :, :, high_rows, :], halo.at[s, :, :, low_halo, :],
-            ysend.at[0], yrecv.at[2 * s], device_id=in_group(1, 0), device_id_type=MESH,
-        ).start()
-        pltpu.make_async_remote_copy(
-            field.at[s, :, :, low_rows, :], halo.at[s, :, :, high_halo, :],
-            ysend.at[1], yrecv.at[2 * s + 1], device_id=in_group(-1, 0), device_id_type=MESH,
         ).start()
     pass_on(0)
 
@@ -240,7 +241,7 @@
         return zpart[rows_of(s, c, x), 0:LANES] + zpart[rows_of(s, c, x), LANES : 2 * LANES]
 
     def local_image(s, carry):
-        def step(g, carry):
+        def step(g, sums):
             layers = [
                 [field[s, c, (g * group + (cx + d)) % cx, own, :] for d in range(-REACH, group + REACH)]
                 for c in range(2)
@@ -256,9 +257,13 @@
                         beside = beside + field[s, c, x, pl.ds(top + k, ry), :]
                         total = total + half_weights[k] * beside
                     image[s, c, x, own, :] = total
-            return carry
-
-        lax.fori_loop(0, cx // group, step, 0)
+                b = [layers[c][i + REACH] for c in range(2)]
+                sums = add_forms(sums, b, b)
+            return sums
+
+        sums = lax.fori_loop(0, cx // group, step, (zero, zero))
+        for c in range(2):
+            partial[c, s] = sums[c]
         return carry
 
     def stage_field(s, carry):
@@ -326,7 +331,7 @@
     inside = [jnp.where(lane >= k, 2.0 * half_weights[k], 0.0) for k in range(1, REACH + 1)]
 
     def inner(s, carry):
-        sums = ((zero, zero),) * 4
+        sums = ((zero, zero),) * 3
         for upper in range(2):
             def pairs(g, sums):
                 for i in range(group):
@@ -344,14 +349,14 @@
                             total = total + inside[k - 1] * pltpu.roll(f, k, 1)
                         w.append(f)
                         once.append(total)
-                    sides = ((b, b), (b, w), (w, w), (w, once))
+                    sides = ((b, w), (w, w), (w, once))
                     sums = tuple(add_forms(old, *pair) for old, pair in zip(sums, sides))
                 return sums
 
             sums = lax.fori_loop(0, half // group, pairs, sums)
-        for i in range(4):
+        for i in range(3):
             for c in range(2):
-                partial[2 * i + c, s] = sums[i][c]
+                partial[2 * i + 2 + c, s] = sums[i][c]
         return carry
 
     lax.fori_loop(0, nsrc, inner, 0)

time: 23.5 us -> 23.4 us (level)
  no operation moved by 1% of the time
where the time goes in v7:
time: 23.4 us; the launch traced here: 23.3 us
  Pallas kernels  21.2 us (91%)
  between operations  1.3 us (6%)
  local copies, waits for them, and re-layouts  0.8 us (3%)
    pallas_call x1, Pallas kernels, per_device(): pl.pallas_call(functools.partial(kernel, ny, nz, nquad), out_shape=jax.Sh...  21.2 us
    unnamed x1, local copies, waits for them, and re-layouts  0.8 us

profile of v7, /device:TPU:1, one launch (start us, length us, event | category | flops | bytes accessed | tf_op | source)
XLA Modules:
  0.0 23.3 jit_solution(9480685213471107329)
XLA Ops:
  1.3 21.2 %shard_map.64 = f32[4,2,4,2,16,128]{5,4,3,2,1,0:T(8,128)S(1)} custom-call(f32[4,16,16,128]{3,2,1,0:T(8,128)} %sr.1, f32[4,16,16,128]{3,2,1,0:T(8,128)} %si.1, f32[16,16,128]{2,1,0:T(8,128)} %pot.1, f32[1]{0:T(128)S(6)} %copy.8.center, f32[1]{0:T(128)S(6)} %copy.9.radius, f32[10,8,128]{2,1,0:T(8,128)} %constant.2.clone.points), custom_call_target="tpu_custom_call" | custom-call | tf_op jit(solution)/shard_map/pallas_call | solution.py:479
  22.5 0.8 %copy.10 = f32[4,2,4,2,16,128]{5,4,3,2,1,0:T(8,128)} copy(f32[4,2,4,2,16,128]{5,4,3,2,1,0:T(8,128)S(1)} %shard_map.64) | data formatting | bytes 1048576

commit v8 on v7

--- a/solution.py
+++ b/solution.py
@@ -95,7 +95,7 @@
     nsrc, cx, ry, _ = sr.shape
     slab = cx // nquad
     half = cx // 2
-    group = 4
+    group = 8
     top = 8
     own = pl.ds(top, ry)
     low_halo, high_halo = pl.ds(top - REACH, REACH), pl.ds(top + ry, REACH)

time: 23.4 us -> 22.9 us (0.979)
  Pallas kernels: 21.2 us -> 20.7 us
    pallas_call x1, Pallas kernels: 21.2 us -> 20.7 us  [per_device(): pl.pallas_call(functools.partial(kernel, ny, nz, nquad), out_shape=jax.Sh...]
where the time goes in v8:
time: 22.9 us; the launch traced here: 22.8 us
  Pallas kernels  20.7 us (90%)
  between operations  1.3 us (6%)
  local copies, waits for them, and re-layouts  0.8 us (3%)
    pallas_call x1, Pallas kernels, per_device(): pl.pallas_call(functools.partial(kernel, ny, nz, nquad), out_shape=jax.Sh...  20.7 us
    unnamed x1, local copies, waits for them, and re-layouts  0.8 us

profile of v8, /device:TPU:1, one launch (start us, length us, event | category | flops | bytes accessed | tf_op | source)
XLA Modules:
  0.0 22.8 jit_solution(5299035105100401951)
XLA Ops:
  1.3 20.7 %shard_map.64 = f32[4,2,4,2,16,128]{5,4,3,2,1,0:T(8,128)S(1)} custom-call(f32[4,16,16,128]{3,2,1,0:T(8,128)} %sr.1, f32[4,16,16,128]{3,2,1,0:T(8,128)} %si.1, f32[16,16,128]{2,1,0:T(8,128)} %pot.1, f32[1]{0:T(128)S(6)} %copy.8.center, f32[1]{0:T(128)S(6)} %copy.9.radius, f32[10,8,128]{2,1,0:T(8,128)} %constant.2.clone.points), custom_call_target="tpu_custom_call" | custom-call | tf_op jit(solution)/shard_map/pallas_call | solution.py:479
  22.0 0.8 %copy.10 = f32[4,2,4,2,16,128]{5,4,3,2,1,0:T(8,128)} copy(f32[4,2,4,2,16,128]{5,4,3,2,1,0:T(8,128)S(1)} %shard_map.64) | data formatting | bytes 1048576
